TPU v7x, 128 devices: a whole 4x4x4 slice. The times are simulated.
128 devices in a mesh: dp: 32 (over x, y, core), fsdp: 4 (over z).
Axes of the slice: x: 4, y: 4, z: 4, core: 2. Of those that a mesh axis runs over, the one named last changes fastest.
Arguments:
- tokens: bfloat16 [32768, 1024], P(('dp', 'fsdp')), may hold values from -6 to 6
- cotangent: bfloat16 [32768, 1024], P(('dp', 'fsdp')), may hold values from -6 to 6
- seg_counts: int32 [32, 3], P('dp'), may hold values from 1 to 1022, as said below
- qkv_master: float32 [1024, 3072], P(('fsdp', 'dp'))
- out_master: float32 [1024, 1024], P(('fsdp', 'dp'))
- up_master: float32 [1024, 4096], P(('fsdp', 'dp'))
- down_master: float32 [4096, 1024], P(('fsdp', 'dp'))
- qkv_first: float32 [1024, 3072], P(('fsdp', 'dp'))
- out_first: float32 [1024, 1024], P(('fsdp', 'dp'))
- up_first: float32 [1024, 4096], P(('fsdp', 'dp'))
- down_first: float32 [4096, 1024], P(('fsdp', 'dp'))
- qkv_second: float32 [1024, 3072], P(('fsdp', 'dp'))
- out_second: float32 [1024, 1024], P(('fsdp', 'dp'))
- up_second: float32 [1024, 4096], P(('fsdp', 'dp'))
- down_second: float32 [4096, 1024], P(('fsdp', 'dp'))
- vec_master: float32 [1024, 12], P(('fsdp', 'dp'))
- vec_first: float32 [1024, 12], P(('fsdp', 'dp'))
- vec_second: float32 [1024, 12], P(('fsdp', 'dp'))
Outputs:
- layer_out: bfloat16 [32768, 1024], P(('dp', 'fsdp'))
- input_grad: bfloat16 [32768, 1024], P(('dp', 'fsdp'))
- qkv_new: float32 [1024, 3072], P(('fsdp', 'dp'))
- out_new: float32 [1024, 1024], P(('fsdp', 'dp'))
- up_new: float32 [1024, 4096], P(('fsdp', 'dp'))
- down_new: float32 [4096, 1024], P(('fsdp', 'dp'))
- qkv_first_new: float32 [1024, 3072], P(('fsdp', 'dp'))
- out_first_new: float32 [1024, 1024], P(('fsdp', 'dp'))
- up_first_new: float32 [1024, 4096], P(('fsdp', 'dp'))
- down_first_new: float32 [4096, 1024], P(('fsdp', 'dp'))
- qkv_second_new: float32 [1024, 3072], P(('fsdp', 'dp'))
- out_second_new: float32 [1024, 1024], P(('fsdp', 'dp'))
- up_second_new: float32 [1024, 4096], P(('fsdp', 'dp'))
- down_second_new: float32 [4096, 1024], P(('fsdp', 'dp'))
- vec_new: float32 [1024, 12], P(('fsdp', 'dp'))
- vec_first_new: float32 [1024, 12], P(('fsdp', 'dp'))
- vec_second_new: float32 [1024, 12], P(('fsdp', 'dp'))
- matrix_norms: float32 [4, 2], replicated
Inputs may be any that keep to these rules, and one draw needn't show every extreme that they name: `seg_counts`: row g holds the patch counts of the 3 images of data group g in the order in which they lie in its 1024 rows, and sums to 1024; its first and last counts are at most 128, and some row reaches that bound in both.
All inputs are finite; a program needn't handle non-finite values.
Results may differ from a plain program's by a relative error of at most 0.013.
The roundings to bfloat16 on the way count: a program that leaves them out, or rounds other values in their place, can miss the bound.
Values may be sent and summed in bfloat16 or wider, within the bound.
No kernel may reach another device: no remote copies, remote signals or barrier semaphores. Data moves between devices by JAX's collectives and lax.ppermute only.
A program may use at most 192 MiB of HBM per device.

v0:
```python
import jax
import jax.numpy as jnp
from jax import lax
from jax.sharding import PartitionSpec as P

HEADS = 16
HEAD_DIM = 64
STEP = 4


LN_EPS = 1e-06
BETA = 0.5
ADAM_EPS = 1e-06
DECAY = 0.01
RATE = 0.5
VEC_RATE = 0.2


def layer_norm(values, gain_vec, shift_vec):
    centre = jnp.mean(values, -1, keepdims=True)
    centred = values - centre
    spread = jnp.mean(centred * centred, -1, keepdims=True)
    return centred * lax.rsqrt(spread + LN_EPS) * gain_vec + shift_vec


def exact_gelu(values):
    return jax.nn.gelu(values, approximate=False)


def segments(counts, places):
    first = counts[0, 0]
    second = first + counts[0, 1]
    return (places >= first).astype(jnp.int32) + (places >= second).astype(jnp.int32)


def masked_scores(query_heads, key_heads, same_image, score_scale):
    raw = (
        jnp.einsum("qhd,khd->hqk", query_heads, key_heads, preferred_element_type=jnp.float32)
        * score_scale
    )
    return jnp.where(same_image, raw, -1e30)


def adam_step(grad_mean, moment, square, weight, decay_rate):
    moment_new = BETA * moment + (1.0 - BETA) * grad_mean
    square_new = BETA * square + (1.0 - BETA) * grad_mean * grad_mean
    correct = 1.0 - BETA**STEP
    direction = (
        moment_new / correct / (jnp.sqrt(square_new / correct) + ADAM_EPS) + decay_rate * weight
    )
    return (moment_new, square_new, direction)


def on_device(
    tokens,
    cotangent,
    seg_counts,
    qkv_master,
    out_master,
    up_master,
    down_master,
    qkv_first,
    out_first,
    up_first,
    down_first,
    qkv_second,
    out_second,
    up_second,
    down_second,
    vec_master,
    vec_first,
    vec_second,
):
    masters = (qkv_master, out_master, up_master, down_master)
    qkv_shard, out_shard, up_shard, down_shard, vec_shard = (
        lax.all_gather(qkv_master.astype(jnp.bfloat16), "dp", axis=0, tiled=True),
        lax.all_gather(out_master.astype(jnp.bfloat16), "dp", axis=0, tiled=True),
        lax.all_gather(up_master.astype(jnp.bfloat16), "dp", axis=0, tiled=True),
        lax.all_gather(down_master.astype(jnp.bfloat16), "dp", axis=0, tiled=True),
        lax.all_gather(vec_master.astype(jnp.bfloat16), "dp", axis=0, tiled=True),
    )
    w_qkv, w_out, vec_full = (
        lax.all_gather(qkv_shard, "fsdp", axis=0, tiled=True),
        lax.all_gather(out_shard, "fsdp", axis=0, tiled=True),
        lax.all_gather(vec_shard, "fsdp", axis=0, tiled=True),
    )
    vectors = vec_full.astype(jnp.float32)
    row_count = tokens.shape[0]
    model_width = tokens.shape[1]
    group_rows = row_count * lax.axis_size("fsdp")
    inputs = tokens.astype(jnp.float32)
    normed = layer_norm(inputs, vectors[:, 0], vectors[:, 1]).astype(jnp.bfloat16)
    qkv_bias = jnp.concatenate(
        [vectors[:, 2], jnp.zeros((model_width,), jnp.float32), vectors[:, 3]]
    )
    qkv_rows = (jnp.dot(normed, w_qkv, preferred_element_type=jnp.float32) + qkv_bias).astype(
        jnp.bfloat16
    )
    key_rows, value_rows = (
        lax.all_gather(qkv_rows[:, model_width : 2 * model_width], "fsdp", axis=0, tiled=True),
        lax.all_gather(qkv_rows[:, 2 * model_width :], "fsdp", axis=0, tiled=True),
    )
    query_heads = qkv_rows[:, :model_width].reshape(row_count, HEADS, HEAD_DIM)
    key_heads = key_rows.reshape(group_rows, HEADS, HEAD_DIM)
    value_heads = value_rows.reshape(group_rows, HEADS, HEAD_DIM)
    own_places = lax.axis_index("fsdp") * row_count + jnp.arange(row_count, dtype=jnp.int32)
    group_places = jnp.arange(group_rows, dtype=jnp.int32)
    same_image = (
        segments(seg_counts, own_places)[:, None] == segments(seg_counts, group_places)[None, :]
    )[None]
    score_scale = HEAD_DIM ** (-0.5)
    scores = masked_scores(query_heads, key_heads, same_image, score_scale)
    row_max = jnp.max(scores, -1, keepdims=True)
    exponent = jnp.exp(scores - row_max)
    row_total = jnp.sum(exponent, -1, keepdims=True)
    probs = exponent / row_total
    log_total = row_max + jnp.log(row_total)
    attended = jnp.einsum(
        "hqk,khd->qhd", probs.astype(jnp.bfloat16), value_heads, preferred_element_type=jnp.float32
    )
    attended = attended.reshape(row_count, model_width).astype(jnp.bfloat16)
    middle = inputs + (jnp.dot(attended, w_out, preferred_element_type=jnp.float32) + vectors[:, 4])
    w_up, w_down = (
        lax.all_gather(up_shard, "fsdp", axis=0, tiled=True),
        lax.all_gather(down_shard, "fsdp", axis=0, tiled=True),
    )
    normed_mid = layer_norm(middle, vectors[:, 5], vectors[:, 6]).astype(jnp.bfloat16)
    up_bias = vectors[:, 7:11].T.reshape(-1)
    pre_act = jnp.dot(normed_mid, w_up, preferred_element_type=jnp.float32) + up_bias
    hidden = exact_gelu(pre_act).astype(jnp.bfloat16)
    layer_out = (
        middle + (jnp.dot(hidden, w_down, preferred_element_type=jnp.float32) + vectors[:, 11])
    ).astype(jnp.bfloat16)
    w_up, w_down = (
        lax.all_gather(up_shard, "fsdp", axis=0, tiled=True),
        lax.all_gather(down_shard, "fsdp", axis=0, tiled=True),
    )
    grad_down = jnp.einsum("tf,td->fd", hidden, cotangent, preferred_element_type=jnp.float32)
    grad_hidden = jnp.einsum("td,fd->tf", cotangent, w_down, preferred_element_type=jnp.float32)
    gelu_value, gelu_back = jax.vjp(exact_gelu, pre_act)
    grad_pre = gelu_back(grad_hidden)[0].astype(jnp.bfloat16)
    grad_up = jnp.einsum("tc,tf->cf", normed_mid, grad_pre, preferred_element_type=jnp.float32)
    grad_normed_mid = jnp.einsum("tf,cf->tc", grad_pre, w_up, preferred_element_type=jnp.float32)
    norm_value, norm_back = jax.vjp(layer_norm, middle, vectors[:, 5], vectors[:, 6])
    grad_from_norm, grad_gain_mid, grad_shift_mid = norm_back(grad_normed_mid)
    grad_middle = cotangent.astype(jnp.float32) + grad_from_norm
    grad_mid_low = grad_middle.astype(jnp.bfloat16)
    w_qkv, w_out = (
        lax.all_gather(qkv_shard, "fsdp", axis=0, tiled=True),
        lax.all_gather(out_shard, "fsdp", axis=0, tiled=True),
    )
    grad_out = jnp.einsum("tc,td->cd", attended, grad_mid_low, preferred_element_type=jnp.float32)
    grad_att = jnp.einsum("td,cd->tc", grad_mid_low, w_out, preferred_element_type=jnp.float32)
    grad_att = grad_att.astype(jnp.bfloat16).reshape(row_count, HEADS, HEAD_DIM)
    probs_again = jnp.exp(
        masked_scores(query_heads, key_heads, same_image, score_scale) - log_total
    )
    grad_probs = jnp.einsum(
        "qhd,khd->hqk", grad_att, value_heads, preferred_element_type=jnp.float32
    )
    row_inner = jnp.sum(probs_again * grad_probs, -1, keepdims=True)
    grad_scores = (probs_again * (grad_probs - row_inner)).astype(jnp.bfloat16)
    grad_query = (
        jnp.einsum("hqk,khd->qhd", grad_scores, key_heads, preferred_element_type=jnp.float32)
        * score_scale
    )
    key_term = (
        jnp.einsum("hqk,qhd->khd", grad_scores, query_heads, preferred_element_type=jnp.float32)
        * score_scale
    )
    value_term = jnp.einsum(
        "hqk,qhd->khd",
        probs_again.astype(jnp.bfloat16),
        grad_att,
        preferred_element_type=jnp.float32,
    )
    grad_key, grad_value = (
        lax.psum_scatter(
            key_term.reshape(group_rows, model_width), "fsdp", scatter_dimension=0, tiled=True
        ),
        lax.psum_scatter(
            value_term.reshape(group_rows, model_width), "fsdp", scatter_dimension=0, tiled=True
        ),
    )
    grad_qkv_rows = jnp.concatenate(
        [
            grad_query.reshape(row_count, model_width).astype(jnp.bfloat16),
            grad_key.astype(jnp.bfloat16),
            grad_value.astype(jnp.bfloat16),
        ],
        axis=1,
    )
    grad_qkv = jnp.einsum("tc,tk->ck", normed, grad_qkv_rows, preferred_element_type=jnp.float32)
    grad_normed = jnp.einsum("tk,ck->tc", grad_qkv_rows, w_qkv, preferred_element_type=jnp.float32)
    first_value, first_back = jax.vjp(layer_norm, inputs, vectors[:, 0], vectors[:, 1])
    grad_from_first, grad_gain_first, grad_shift_first = first_back(grad_normed)
    input_grad = (grad_middle + grad_from_first).astype(jnp.bfloat16)
    bias_sums = jnp.sum(grad_qkv_rows, axis=0, dtype=jnp.float32)
    small_columns = jnp.stack(
        [
            grad_gain_first,
            grad_shift_first,
            bias_sums[:model_width],
            bias_sums[2 * model_width :],
            jnp.sum(grad_mid_low, axis=0, dtype=jnp.float32),
            grad_gain_mid,
            grad_shift_mid,
        ],
        axis=1,
    )
    up_columns = jnp.sum(grad_pre, axis=0, dtype=jnp.float32).reshape(4, model_width).T
    down_column = jnp.sum(cotangent, axis=0, dtype=jnp.float32)[:, None]
    vec_grad = jnp.concatenate([small_columns, up_columns, down_column], axis=1)
    data_count = lax.axis_size("dp")
    qkv_summed, out_summed, up_summed, down_summed, vec_summed = (
        lax.psum_scatter(grad_qkv, "fsdp", scatter_dimension=0, tiled=True),
        lax.psum_scatter(grad_out, "fsdp", scatter_dimension=0, tiled=True),
        lax.psum_scatter(grad_up, "fsdp", scatter_dimension=0, tiled=True),
        lax.psum_scatter(grad_down, "fsdp", scatter_dimension=0, tiled=True),
        lax.psum_scatter(vec_grad, "fsdp", scatter_dimension=0, tiled=True),
    )
    reduced = (
        lax.psum_scatter(qkv_summed, "dp", scatter_dimension=0, tiled=True),
        lax.psum_scatter(out_summed, "dp", scatter_dimension=0, tiled=True),
        lax.psum_scatter(up_summed, "dp", scatter_dimension=0, tiled=True),
        lax.psum_scatter(down_summed, "dp", scatter_dimension=0, tiled=True),
        lax.psum_scatter(vec_summed, "dp", scatter_dimension=0, tiled=True),
    )
    firsts = (qkv_first, out_first, up_first, down_first)
    seconds = (qkv_second, out_second, up_second, down_second)
    results = [
        adam_step(grad_sum / data_count, moment, square, weight, DECAY)
        for grad_sum, moment, square, weight in zip(reduced[:4], firsts, seconds, masters)
    ]
    update_local = jnp.stack([jnp.sum(parts[2] * parts[2]) for parts in results])
    weight_sq, update_sq = lax.psum(
        (jnp.stack([jnp.sum(matrix * matrix) for matrix in masters]), update_local), ("dp", "fsdp")
    )
    weight_norm = jnp.sqrt(weight_sq)
    update_norm = jnp.sqrt(update_sq)
    ratio = weight_norm / update_norm
    new_mats = [
        weight - RATE * ratio[place] * parts[2]
        for place, (weight, parts) in enumerate(zip(masters, results))
    ]
    vec_moment, vec_square, vec_dir = adam_step(
        reduced[4] / data_count, vec_first, vec_second, vec_master, 0.0
    )
    vec_new = vec_master - VEC_RATE * vec_dir
    matrix_norms = jnp.stack([weight_norm, update_norm], axis=1)
    return (
        layer_out,
        input_grad,
        new_mats[0],
        new_mats[1],
        new_mats[2],
        new_mats[3],
        results[0][0],
        results[1][0],
        results[2][0],
        results[3][0],
        results[0][1],
        results[1][1],
        results[2][1],
        results[3][1],
        vec_new,
        vec_moment,
        vec_square,
        matrix_norms,
    )


def solution(mesh):
    return jax.shard_map(
        on_device,
        mesh=mesh,
        in_specs=(
            P(("dp", "fsdp"), None),
            P(("dp", "fsdp"), None),
            P("dp", None),
            P(("fsdp", "dp"), None),
            P(("fsdp", "dp"), None),
            P(("fsdp", "dp"), None),
            P(("fsdp", "dp"), None),
            P(("fsdp", "dp"), None),
            P(("fsdp", "dp"), None),
            P(("fsdp", "dp"), None),
            P(("fsdp", "dp"), None),
            P(("fsdp", "dp"), None),
            P(("fsdp", "dp"), None),
            P(("fsdp", "dp"), None),
            P(("fsdp", "dp"), None),
            P(("fsdp", "dp"), None),
            P(("fsdp", "dp"), None),
            P(("fsdp", "dp"), None),
        ),
        out_specs=(
            P(("dp", "fsdp"), None),
            P(("dp", "fsdp"), None),
            P(("fsdp", "dp"), None),
            P(("fsdp", "dp"), None),
            P(("fsdp", "dp"), None),
            P(("fsdp", "dp"), None),
            P(("fsdp", "dp"), None),
            P(("fsdp", "dp"), None),
            P(("fsdp", "dp"), None),
            P(("fsdp", "dp"), None),
            P(("fsdp", "dp"), None),
            P(("fsdp", "dp"), None),
            P(("fsdp", "dp"), None),
            P(("fsdp", "dp"), None),
            P(("fsdp", "dp"), None),
            P(("fsdp", "dp"), None),
            P(("fsdp", "dp"), None),
            P(),
        ),
        check_vma=False,
    )
```

profile of v0, /device:TPU:0, one launch (start us, length us, event | category | flops | bytes accessed | tf_op | source)
XLA Modules:
  0.0 1527.3 jit_solution(3150726173618917091)
XLA Ops:
  8.9 47.6 %all-gather.10.cloned.1.call-done = bf16[256,3072]{1,0:T(8,128)(2,1)} async-done(((bf16[8,3072]{1,0:T(8,128)(2,1)}), bf16[256,3072]{1,0:T(8,128)(2,1)}) %all-gather.10.cloned.1.call-update) | async-done | bytes 1572880 | tf_op jit(solution)/shard_map/all_gather | solution.py:76
  60.5 23.4 %all_gather.40 = bf16[256,12]{1,0:T(8,128)(2,1)S(1)} all-gather(bf16[8,12]{1,0:T(8,128)(2,1)S(1)} %convert_element_type.123), channel_id=1, replica_groups=mesh['dp'=32,'fsdp'=4] {'dp'}, dimensions={0}, use_global_device_ids=true | all-gather | bytes 6336 | tf_op jit(solution)/shard_map/all_gather | solution.py:80
  83.9 13.8 all_gather.41
  100.4 25.2 %all-gather.12.cloned.1.call-done = bf16[1024,3072]{1,0:T(8,128)(2,1)} async-done(((bf16[256,3072]{1,0:T(8,128)(2,1)}), bf16[1024,3072]{1,0:T(8,128)(2,1)}) %all-gather.12.cloned.1.call-update) | async-done | bytes 6291472 | tf_op jit(solution)/shard_map/all_gather | solution.py:83
  125.6 4.7 fusion.12
  132.1 27.0 %all_gather.46 = bf16[256,1024]{1,0:T(8,128)(2,1)} all-gather(bf16[8,1024]{1,0:T(8,128)(2,1)S(1)} %convert_element_type.136), channel_id=1, replica_groups=mesh['dp'=32,'fsdp'=4] {'dp'}, dimensions={0}, use_global_device_ids=true | all-gather | bytes 540672 | tf_op jit(solution)/shard_map/all_gather | solution.py:77
  159.2 13.5 all-gather.20.cloned.1.call-done
  172.7 45.6 %all-gather.24.cloned.1.call-done = bf16[1024,1024]{1,0:T(8,128)(2,1)} async-done(((bf16[32,1024]{1,0:T(8,128)(2,1)}), bf16[1024,1024]{1,0:T(8,128)(2,1)}) %all-gather.24.cloned.1.call-update) | async-done | bytes 2097168 | tf_op jit(solution)/shard_map/all_gather | solution.py:79
  222.9 27.9 %all-gather.16.cloned.1.call-done = bf16[1024,1024]{1,0:T(8,128)(2,1)} async-done(((bf16[256,1024]{1,0:T(8,128)(2,1)}), bf16[1024,1024]{1,0:T(8,128)(2,1)}) %all-gather.16.cloned.1.call-update) | async-done | bytes 2097168 | tf_op jit(solution)/shard_map/all_gather | solution.py:100
  250.8 2.9 copy.70
  253.7 30.2 %all-gather.14.cloned.1.call-done = bf16[1024,1024]{1,0:T(8,128)(2,1)} async-done(((bf16[256,1024]{1,0:T(8,128)(2,1)}), bf16[1024,1024]{1,0:T(8,128)(2,1)}) %all-gather.14.cloned.1.call-update) | async-done | bytes 2097168 | tf_op jit(solution)/shard_map/all_gather | solution.py:101
  283.8 3.9 copy.68
  287.8 3.0 fusion.46
  290.9 3.8 fusion
  294.7 3.0 copy-done
  297.7 4.3 fusion.20
  302.0 14.5 all-gather.18.cloned.1.call-done
  316.5 2.4 fusion.47
  319.2 82.2 %all-gather.22.cloned.1.call-done = bf16[1024,4096]{1,0:T(8,128)(2,1)} async-done(((bf16[256,4096]{1,0:T(8,128)(2,1)}), bf16[1024,4096]{1,0:T(8,128)(2,1)}) %all-gather.22.cloned.1.call-update) | async-done | bytes 8388624 | tf_op jit(solution)/shard_map/all_gather | solution.py:124
  401.4 7.8 convolution_add_fusion
  409.2 78.0 %all-gather.26.cloned.1.call-done = bf16[4096,1024]{1,0:T(8,128)(2,1)} async-done(((bf16[1024,1024]{1,0:T(8,128)(2,1)}), bf16[4096,1024]{1,0:T(8,128)(2,1)}) %all-gather.26.cloned.1.call-update) | async-done | bytes 8388624 | tf_op jit(solution)/shard_map/all_gather | solution.py:125
  487.3 16.8 %convert_reduce_fusion = (f32[4096]{0:T(1024)}, bf16[256,4096]{1,0:T(8,128)(2,1)S(1)}, f32[256,4096]{1,0:T(8,128)}) fusion(f32[256,4096]{1,0:T(8,128)} %convolution_add_fusion, bf16[256,1024]{1,0:T(8,128)(2,1)S(1)} %copy-done.14, bf16[4096,1024]{1,0:T(8,128)(2,1)} %all-gather.26.cloned.1.call-done), kind=kOutput, calls=%fused_computation.14 | convolution fusion | flops 2225074176 | bytes 19415040 | tf_op jit(solution)/shard_map/td,fd->tf/dot_general | solution.py:139
  505.4 3.2 multiply_reduce_fusion.1
  511.6 9.6 fusion.2
  521.3 9.8 multiply_reduce_fusion
  531.1 7.9 multiply_convert_fusion
  539.1 4.1 convolution_multiply_fusion
  544.9 2.8 fusion.48
  549.2 6.9 fusion.19
  556.1 13.1 reduce-scatter.15.cloned.1.call-done
  570.5 47.9 %reduce-scatter.13.cloned.1.call-done = f32[256,1024]{0,1:T(8,128)} async-done(((f32[1024,1024]{0,1:T(8,128)}), f32[256,1024]{0,1:T(8,128)}) %reduce-scatter.13.cloned.1.call-update) | async-done | bytes 1048592 | tf_op jit(solution)/shard_map/reduce_scatter | solution.py:178
  619.7 7.8 fusion.32
  628.8 10.2 fusion.37
  639.3 4.3 multiply_convert_fusion.1
  644.9 8.1 fusion.49
  654.7 5.2 fusion.38
  661.9 3.5 concatenate.11
  667.4 116.9 %reduce-scatter.17.cloned.1.call-done = f32[256,3072]{1,0:T(8,128)} async-done(((f32[1024,3072]{1,0:T(8,128)}), f32[256,3072]{1,0:T(8,128)}) %reduce-scatter.17.cloned.1.call-update) | async-done | bytes 3145744 | tf_op jit(solution)/shard_map/reduce_scatter | solution.py:216
  784.3 150.1 %reduce-scatter.25.cloned.1.call-done = f32[256,4096]{1,0:T(8,128)} async-done(((f32[1024,4096]{1,0:T(8,128)}), f32[256,4096]{1,0:T(8,128)}) %reduce-scatter.25.cloned.1.call-update) | async-done | bytes 4194320 | tf_op jit(solution)/shard_map/reduce_scatter | solution.py:218
  934.5 150.0 %reduce-scatter.29.cloned.1.call-done = f32[1024,1024]{1,0:T(8,128)} async-done(((f32[4096,1024]{1,0:T(8,128)}), f32[1024,1024]{1,0:T(8,128)}) %reduce-scatter.29.cloned.1.call-update) | async-done | bytes 4194320 | tf_op jit(solution)/shard_map/reduce_scatter | solution.py:219
  1085.9 6.6 fusion.18
  1092.5 15.1 reduce-scatter.33.cloned.1.call-done
  1107.5 125.8 %all-reduce = f32[256,12]{0,1:T(8,128)S(1)} all-reduce(f32[256,12]{0,1:T(8,128)} %reduce-scatter.33.cloned.1.call-done), channel_id=13, replica_groups=mesh['dp'=32,'fsdp'=4] {'dp'}, use_global_device_ids=true, to_apply=%region_40.41.clone | all-reduce | flops 3072 | bytes 24576
  1235.6 36.0 %reduce-scatter.19.cloned.1.call-done = f32[8,3072]{1,0:T(8,128)} async-done(((f32[256,3072]{1,0:T(8,128)}), f32[8,3072]{1,0:T(8,128)}) %reduce-scatter.19.cloned.1.call-update) | async-done | bytes 98320 | tf_op jit(solution)/shard_map/reduce_scatter | solution.py:223
  1273.3 83.2 %reduce-scatter.27.cloned.1.call-done = f32[8,4096]{1,0:T(8,128)} async-done(((f32[256,4096]{1,0:T(8,128)}), f32[8,4096]{1,0:T(8,128)}) %reduce-scatter.27.cloned.1.call-update) | async-done | bytes 131088 | tf_op jit(solution)/shard_map/reduce_scatter | solution.py:225
  1358.3 83.4 %reduce-scatter.31.cloned.1.call-done = f32[32,1024]{1,0:T(8,128)} async-done(((f32[1024,1024]{1,0:T(8,128)}), f32[32,1024]{1,0:T(8,128)}) %reduce-scatter.31.cloned.1.call-update) | async-done | bytes 131088 | tf_op jit(solution)/shard_map/reduce_scatter | solution.py:226
  1443.4 5.2 pad_maximum_fusion.3
  1448.5 64.8 %all-reduce.1 = (f32[4]{0:T(128)S(1)}, f32[4]{0:T(128)S(1)}) all-reduce(f32[4]{0:T(128)S(1)} %get-tuple-element.122, f32[4]{0:T(128)S(1)} %get-tuple-element.121), channel_id=1, replica_groups=mesh['dp'=32,'fsdp'=4] {'dp','fsdp'}, use_global_device_ids=true, to_apply=%region_30.31 | all-reduce | flops 8 | bytes 64 | tf_op jit(solution)/shard_map/psum | solution.py:236
  (225 shorter events, 44.4 us)
Async XLA Ops:
  7.2 92.7 %copy-start.2 = (bf16[256,1024]{1,0:T(8,128)(2,1)S(1)}, bf16[256,1024]{1,0:T(8,128)(2,1)}, u32[]{:S(2)}) copy-start(bf16[256,1024]{1,0:T(8,128)(2,1)} %param.18) | copy-start | bytes 1572868
  7.2 49.3 %all-gather.10.cloned.1.call-start = ((), (), s32[]{:S(2)}) async-start(), calls=%async_computation.11 | async-start | bytes 1622016 | tf_op jit(solution)/shard_map/all_gather | solution.py:76
  8.8 116.7 %all-gather.12.cloned.1.call-start = ((), (), s32[]{:S(2)}) async-start(), calls=%async_computation.12 | async-start | bytes 7864320 | tf_op jit(solution)/shard_map/all_gather | solution.py:83
  56.5 116.2 %all-gather.20.cloned.1.call-start = ((), (), s32[]{:S(2)}) async-start(), calls=%async_computation.16 | async-start | bytes 2162688 | tf_op jit(solution)/shard_map/all_gather | solution.py:78
  58.1 160.2 %all-gather.24.cloned.1.call-start = ((), (), s32[]{:S(2)}) async-start(), calls=%async_computation.18 | async-start | bytes 2162688 | tf_op jit(solution)/shard_map/all_gather | solution.py:79
  59.7 191.1 %all-gather.16.cloned.1.call-start = ((), (), s32[]{:S(2)}) async-start(), calls=%async_computation.14 | async-start | bytes 2621440 | tf_op jit(solution)/shard_map/all_gather | solution.py:100
  99.9 301.5 %copy-start.37 = (f32[1024]{0:T(1024)}, f32[1024]{0:T(1024)S(1)}, u32[]{:S(2)}) copy-start(f32[1024]{0:T(1024)S(1)} %get-tuple-element.62) | copy-start | bytes 12292
  131.4 87.8 %copy-start.61 = (s32[1,3]{1,0:T(1,128)S(1)}, s32[1,3]{1,0:T(1,128)}, u32[]{:S(2)}) copy-start(s32[1,3]{1,0:T(1,128)} %param.20) | copy-start | bytes 40
  131.5 152.4 %all-gather.14.cloned.1.call-start = ((), (), s32[]{:S(2)}) async-start(), calls=%async_computation.13 | async-start | bytes 2621440 | tf_op jit(solution)/shard_map/all_gather | solution.py:101
  132.0 184.4 %all-gather.18.cloned.1.call-start = ((), (), s32[]{:S(2)}) async-start(), calls=%async_computation.15 | async-start | bytes 2621440 | tf_op jit(solution)/shard_map/all_gather | solution.py:84
  159.1 242.3 %all-gather.22.cloned.1.call-start = ((), (), s32[]{:S(2)}) async-start(), calls=%async_computation.17 | async-start | bytes 10485760 | tf_op jit(solution)/shard_map/all_gather | solution.py:124
  172.7 314.6 %all-gather.26.cloned.1.call-start = ((), (), s32[]{:S(2)}) async-start(), calls=%async_computation.19 | async-start | bytes 10485760 | tf_op jit(solution)/shard_map/all_gather | solution.py:125
  218.3 350.9 %reduce-scatter.15.cloned.1.call-start = ((), (), s32[]{:S(2)}) async-start(), calls=%async_computation.21 | async-start | bytes 5242880 | tf_op jit(solution)/shard_map/reduce_scatter | solution.py:181
  302.0 99.4 %copy-start.19 = (bf16[16,64,256]{2,1,0:T(8,128)(2,1)}, bf16[16,64,256]{2,1,0:T(8,128)(2,1)S(1)}, u32[]{:S(2)}) copy-start(bf16[16,64,256]{2,1,0:T(8,128)(2,1)S(1)} %fusion.20) | copy-start | bytes 1572868
  318.9 189.7 %copy-start.5 = (f32[256,1024]{1,0:T(8,128)}, f32[256,1024]{1,0:T(8,128)S(1)}, u32[]{:S(2)}) copy-start(f32[256,1024]{1,0:T(8,128)S(1)} %get-tuple-element.116) | copy-start | bytes 3145732
  318.9 189.7 %copy-start.45 = (f32[256]{0:T(256)}, f32[256]{0:T(256)S(1)}, u32[]{:S(2)}) copy-start(f32[256]{0:T(256)S(1)} %broadcast_multiply_fusion) | copy-start | bytes 3076
  319.2 189.4 %copy-start.47 = (f32[256]{0:T(256)}, f32[256]{0:T(256)S(1)}, u32[]{:S(2)}) copy-start(f32[256]{0:T(256)S(1)} %fusion.31) | copy-start | bytes 3076
  319.2 192.4 %copy-start.36 = (f32[16,256]{1,0:T(8,128)}, f32[16,256]{1,0:T(8,128)S(1)}, u32[]{:S(2)}) copy-start(f32[16,256]{1,0:T(8,128)S(1)} %log_add_fusion) | copy-start | bytes 49156
  401.4 85.9 %copy-start.14 = (bf16[256,1024]{1,0:T(8,128)(2,1)S(1)}, bf16[256,1024]{1,0:T(8,128)(2,1)}, u32[]{:S(2)}) copy-start(bf16[256,1024]{1,0:T(8,128)(2,1)} %param.19) | copy-start | bytes 1572868
  521.3 97.2 %reduce-scatter.13.cloned.1.call-start = ((), (), s32[]{:S(2)}) async-start(), calls=%async_computation.20 | async-start | bytes 5242880 | tf_op jit(solution)/shard_map/reduce_scatter | solution.py:178
  543.7 123.6 %reduce-scatter.21.cloned.1.call-start = ((), (), s32[]{:S(2)}) async-start(), calls=%async_computation.24 | async-start | bytes 5242880 | tf_op jit(solution)/shard_map/reduce_scatter | solution.py:217
  547.7 72.1 %copy-start.42 = (f32[256]{0:T(256)S(1)}, f32[256]{0:T(256)}, u32[]{:S(2)}) copy-start(f32[256]{0:T(256)} %copy-done.41) | copy-start | bytes 3076
  547.7 236.6 %reduce-scatter.17.cloned.1.call-start = ((), (), s32[]{:S(2)}) async-start(), calls=%async_computation.22 | async-start | bytes 15728640 | tf_op jit(solution)/shard_map/reduce_scatter | solution.py:216
  627.6 306.9 %reduce-scatter.25.cloned.1.call-start = ((), (), s32[]{:S(2)}) async-start(), calls=%async_computation.26 | async-start | bytes 20971520 | tf_op jit(solution)/shard_map/reduce_scatter | solution.py:218
  639.0 445.5 %reduce-scatter.29.cloned.1.call-start = ((), (), s32[]{:S(2)}) async-start(), calls=%async_computation.28 | async-start | bytes 20971520 | tf_op jit(solution)/shard_map/reduce_scatter | solution.py:219
  653.1 454.5 %reduce-scatter.33.cloned.1.call-start = ((), (), s32[]{:S(2)}) async-start(), calls=%async_computation.30 | async-start | bytes 81920 | tf_op jit(solution)/shard_map/reduce_scatter | solution.py:220
  665.4 568.7 %reduce-scatter.23.cloned.1.call-start = ((), (), s32[]{:S(2)}) async-start(), calls=%async_computation.25 | async-start | bytes 1081344 | tf_op jit(solution)/shard_map/reduce_scatter | solution.py:224
  667.3 604.3 %reduce-scatter.19.cloned.1.call-start = ((), (), s32[]{:S(2)}) async-start(), calls=%async_computation.23 | async-start | bytes 3244032 | tf_op jit(solution)/shard_map/reduce_scatter | solution.py:223
  784.3 572.2 %reduce-scatter.27.cloned.1.call-start = ((), (), s32[]{:S(2)}) async-start(), calls=%async_computation.27 | async-start | bytes 4325376 | tf_op jit(solution)/shard_map/reduce_scatter | solution.py:225
  934.5 150.1 %copy-start.63 = (u32[128]{0:T(128)S(1)}, u32[128]{0:T(128)}, u32[]{:S(2)}) copy-start(u32[128]{0:T(128)} %constant.167) | copy-start | bytes 1540
  934.5 151.3 %copy-start.10 = (bf16[256,4096]{1,0:T(8,128)(2,1)S(1)}, bf16[256,4096]{1,0:T(8,128)(2,1)}, u32[]{:S(2)}) copy-start(bf16[256,4096]{1,0:T(8,128)(2,1)} %copy-done.9) | copy-start | bytes 6291460
  934.5 151.4 %copy-start.60 = (f32[1024]{0:T(1024)S(1)}, f32[1024]{0:T(1024)}, u32[]{:S(2)}) copy-start(f32[1024]{0:T(1024)} %get-tuple-element.61) | copy-start | bytes 12292
  934.5 507.1 %reduce-scatter.31.cloned.1.call-start = ((), (), s32[]{:S(2)}) async-start(), calls=%async_computation.29 | async-start | bytes 4325376 | tf_op jit(solution)/shard_map/reduce_scatter | solution.py:226
  1085.8 147.7 %copy-start.50 = (f32[8,12]{1,0:T(8,128)S(1)}, f32[8,12]{1,0:T(8,128)}, u32[]{:S(2)}) copy-start(f32[8,12]{1,0:T(8,128)} %param.33) | copy-start | bytes 1156
  1085.8 147.7 %copy-start.56 = (f32[8,12]{1,0:T(8,128)S(1)}, f32[8,12]{1,0:T(8,128)}, u32[]{:S(2)}) copy-start(f32[8,12]{1,0:T(8,128)} %param.34) | copy-start | bytes 1156
  1085.8 147.7 %copy-start.57 = (f32[8,12]{1,0:T(8,128)S(1)}, f32[8,12]{1,0:T(8,128)}, u32[]{:S(2)}) copy-start(f32[8,12]{1,0:T(8,128)} %param.35) | copy-start | bytes 1156
  1085.9 148.3 %copy-start.35 = (f32[8,1024]{1,0:T(8,128)S(1)}, f32[8,1024]{1,0:T(8,128)}, u32[]{:S(2)}) copy-start(f32[8,1024]{1,0:T(8,128)} %param.22) | copy-start | bytes 98308
  1085.9 185.7 %copy-start.27 = (f32[8,3072]{1,0:T(8,128)S(1)}, f32[8,3072]{1,0:T(8,128)}, u32[]{:S(2)}) copy-start(f32[8,3072]{1,0:T(8,128)} %param.21) | copy-start | bytes 294916
  1085.9 270.6 %copy-start.26 = (f32[8,4096]{1,0:T(8,128)S(1)}, f32[8,4096]{1,0:T(8,128)}, u32[]{:S(2)}) copy-start(f32[8,4096]{1,0:T(8,128)} %param.23) | copy-start | bytes 393220
  1085.9 355.7 %copy-start.25 = (f32[32,1024]{1,0:T(8,128)S(1)}, f32[32,1024]{1,0:T(8,128)}, u32[]{:S(2)}) copy-start(f32[32,1024]{1,0:T(8,128)} %param.24) | copy-start | bytes 393220
  1235.6 284.3 %copy-start.39 = (f32[8,1024]{1,0:T(8,128)}, f32[8,1024]{1,0:T(8,128)S(1)}, u32[]{:S(2)}) copy-start(f32[8,1024]{1,0:T(8,128)S(1)} %get-tuple-element.89) | copy-start | bytes 98308
  1235.6 284.3 %copy-start.40 = (f32[8,1024]{1,0:T(8,128)}, f32[8,1024]{1,0:T(8,128)S(1)}, u32[]{:S(2)}) copy-start(f32[8,1024]{1,0:T(8,128)S(1)} %get-tuple-element.90) | copy-start | bytes 98308
  1273.3 246.6 %copy-start.32 = (f32[8,3072]{1,0:T(8,128)}, f32[8,3072]{1,0:T(8,128)S(1)}, u32[]{:S(2)}) copy-start(f32[8,3072]{1,0:T(8,128)S(1)} %get-tuple-element.87) | copy-start | bytes 294916
  1273.3 246.6 %copy-start.33 = (f32[8,3072]{1,0:T(8,128)}, f32[8,3072]{1,0:T(8,128)S(1)}, u32[]{:S(2)}) copy-start(f32[8,3072]{1,0:T(8,128)S(1)} %get-tuple-element.88) | copy-start | bytes 294916
  1358.3 161.7 %copy-start.28 = (f32[8,4096]{1,0:T(8,128)}, f32[8,4096]{1,0:T(8,128)S(1)}, u32[]{:S(2)}) copy-start(f32[8,4096]{1,0:T(8,128)S(1)} %get-tuple-element.91) | copy-start | bytes 393220
  1358.3 161.7 %copy-start.29 = (f32[8,4096]{1,0:T(8,128)}, f32[8,4096]{1,0:T(8,128)S(1)}, u32[]{:S(2)}) copy-start(f32[8,4096]{1,0:T(8,128)S(1)} %get-tuple-element.92) | copy-start | bytes 393220
  1443.4 76.6 %copy-start.30 = (f32[32,1024]{1,0:T(8,128)}, f32[32,1024]{1,0:T(8,128)S(1)}, u32[]{:S(2)}) copy-start(f32[32,1024]{1,0:T(8,128)S(1)} %get-tuple-element.93) | copy-start | bytes 393220
  1443.4 76.6 %copy-start.31 = (f32[32,1024]{1,0:T(8,128)}, f32[32,1024]{1,0:T(8,128)S(1)}, u32[]{:S(2)}) copy-start(f32[32,1024]{1,0:T(8,128)S(1)} %get-tuple-element.94) | copy-start | bytes 393220
  (36 other events, 360.0 us)
Sparse Core Ops, SparseCore 0:
  10.9 45.5 all-gather.9
  58.1 67.3 all-gather.11
  128.4 44.1 all-gather.19
  175.3 42.9 all-gather.23
  220.4 30.3 all-gather.15
  252.9 30.9 all-gather.13
  285.5 30.9 all-gather.17
  318.1 83.2 all-gather.21
  403.1 84.1 all-gather.25
  521.4 47.8 reduce-scatter.14
  571.8 46.6 reduce-scatter.12
  620.7 46.5 reduce-scatter.20
  669.9 114.3 reduce-scatter.16
  786.7 147.6 reduce-scatter.24
  936.8 147.7 reduce-scatter.28
  1087.4 20.0 reduce-scatter.32
  1110.9 77.0 reduce-scatter.22
  1191.9 79.6 reduce-scatter.18
  1275.3 81.2 reduce-scatter.26
  1360.4 81.1 reduce-scatter.30
where the time goes:
time: 1530 us
  waiting for transfers between devices  1060 us (69%)
  blocking collectives  255 us (17%)
  matrix products  114 us (7%)
  other arithmetic  45.7 us (3%)
  local copies, waits for them, and re-layouts  28.2 us (2%)
  between operations  20.1 us (1%)
    reduce_scatter x1, waiting for transfers between devices, on_device(): lax.psum_scatter(grad_up, 'fsdp', scatter_dimension=0, tiled=True)  150 us
    reduce_scatter x1, waiting for transfers between devices, on_device(): lax.psum_scatter(grad_down, 'fsdp', scatter_dimension=0, tiled=True)  150 us
    unnamed x1, blocking collectives  126 us
    reduce_scatter x1, waiting for transfers between devices, on_device(): lax.psum_scatter(grad_qkv, 'fsdp', scatter_dimension=0, tiled=True)  117 us
    reduce_scatter x1, waiting for transfers between devices, on_device(): lax.psum_scatter(down_summed, 'dp', scatter_dimension=0, tiled=True)  83.4 us
    reduce_scatter x1, waiting for transfers between devices, on_device(): lax.psum_scatter(up_summed, 'dp', scatter_dimension=0, tiled=True)  83.2 us
    all_gather x1, waiting for transfers between devices, on_device(): lax.all_gather(up_shard, 'fsdp', axis=0, tiled=True)  82.2 us
    all_gather x1, waiting for transfers between devices, on_device(): lax.all_gather(down_shard, 'fsdp', axis=0, tiled=True)  78 us
  transfers between devices with their start and end apart: 20, of which 19 were waited for; matrix products, arithmetic and copies ran while one was open for 9% of the time, Pallas kernels for 0%

commit v1 on v0

v1 whole, which is shorter than its diff:
```python
import jax
import jax.numpy as jnp
from jax import lax
from jax.sharding import Mesh
from jax.sharding import PartitionSpec as P

HEADS = 16
HEAD_DIM = 64
STEP = 4

LN_EPS = 1e-06
BETA = 0.5
ADAM_EPS = 1e-06
DECAY = 0.01
RATE = 0.5
VEC_RATE = 0.2

LOW = jnp.bfloat16
WIDE = jnp.float32
DATA = ("x", "y", "c")
EVERY = ("x", "y", "c", "z")
RING = 4
VEC_PAD = 128


def send(block, axis, step):
    size = lax.axis_size(axis)
    return lax.ppermute(block, axis, [(i, (i + step) % size) for i in range(size)])


def gather_z(block):
    half = block.shape[0] // 2
    from_prev = send(block, "z", 1)
    from_next = send(block, "z", -1)
    far = jnp.concatenate([send(from_prev[:half], "z", 1), send(from_next[half:], "z", -1)])
    return jnp.concatenate([block, from_next, far, from_prev])


def scatter_z(partial):
    rows = partial.shape[0] // RING
    half = rows // 2
    own, after, far, before = (partial[k * rows : (k + 1) * rows] for k in range(RING))
    far = far.astype(LOW)
    from_prev = send(far[:half], "z", 1).astype(WIDE)
    from_next = send(far[half:], "z", -1).astype(WIDE)
    after = jnp.concatenate([after[:half] + from_prev, after[half:]])
    before = jnp.concatenate([before[:half], before[half:] + from_next])
    return (
        own
        + send(after.astype(LOW), "z", 1).astype(WIDE)
        + send(before.astype(LOW), "z", -1).astype(WIDE)
    )


def swap_z(pieces):
    place = lax.axis_index("z")

    def piece(step):
        return lax.dynamic_index_in_dim(pieces, (place + step) % RING, 0, keepdims=False)

    arrived = jnp.stack([piece(0), send(piece(3), "z", 3), send(piece(2), "z", 2), send(piece(1), "z", 1)])
    return jnp.roll(arrived, place, axis=0)


def sum_everywhere(values):
    for axis in ("c", "x", "y", "z"):
        size = lax.axis_size(axis)
        apart = 1
        while apart < size:
            values = values + lax.ppermute(values, axis, [(i, i ^ apart) for i in range(size)])
            apart *= 2
    return values


def normalise(values):
    centre = jnp.mean(values, -1, keepdims=True)
    centred = values - centre
    spread = jnp.mean(centred * centred, -1, keepdims=True)
    scale = lax.rsqrt(spread + LN_EPS)
    return centred * scale, scale


def normalise_back(grad, unit, scale, gain):
    grad_unit = grad * gain
    return scale * (
        grad_unit
        - jnp.mean(grad_unit, -1, keepdims=True)
        - unit * jnp.mean(grad_unit * unit, -1, keepdims=True)
    )


def adam_step(grad_mean, moment, square, weight, decay_rate):
    moment_new = BETA * moment + (1.0 - BETA) * grad_mean
    square_new = BETA * square + (1.0 - BETA) * grad_mean * grad_mean
    correct = 1.0 - BETA**STEP
    direction = (
        moment_new / correct / (jnp.sqrt(square_new / correct) + ADAM_EPS) + decay_rate * weight
    )
    return (moment_new, square_new, direction)


def dot(left, right, dims):
    return lax.dot_general(left, right, (dims, ((), ())), preferred_element_type=WIDE)


def on_device(
    tokens,
    cotangent,
    seg_counts,
    qkv_master,
    out_master,
    up_master,
    down_master,
    qkv_first,
    out_first,
    up_first,
    down_first,
    qkv_second,
    out_second,
    up_second,
    down_second,
    vec_master,
    vec_first,
    vec_second,
):
    masters = (qkv_master, out_master, up_master, down_master)
    place = lax.axis_index("z")
    rows, width = tokens.shape
    own = qkv_master.shape[0]
    lanes = width // RING
    hidden_lanes = up_master.shape[1] // RING
    data = lax.axis_size("x") * lax.axis_size("y") * lax.axis_size("c")
    heads = HEADS // RING
    group = rows * RING

    qkv_parts = (
        qkv_master.astype(LOW)
        .reshape(own, 3, RING, lanes)
        .transpose(2, 0, 1, 3)
        .reshape(RING, own, 3 * lanes)
    )
    vec_low = jnp.pad(vec_master.astype(LOW), ((0, 0), (0, VEC_PAD - vec_master.shape[1])))
    up_parts = up_master.astype(LOW).reshape(own, RING, hidden_lanes).transpose(1, 0, 2)
    weight_parts = jnp.concatenate(
        [qkv_parts, jnp.broadcast_to(vec_low, (RING, own, VEC_PAD)), up_parts], axis=2
    )
    arrived = swap_z(weight_parts)
    att_columns = 3 * lanes + VEC_PAD
    first_pack = lax.all_gather(arrived[:, :, :att_columns], DATA, axis=0)
    first_pack = first_pack.transpose(1, 0, 2, 3).reshape(width, att_columns)
    w_qkv = first_pack[:, : 3 * lanes]
    vectors = first_pack[:, 3 * lanes : 3 * lanes + vec_master.shape[1]].astype(WIDE)

    inputs = gather_z(tokens)
    w_out = lax.all_gather(out_master.astype(LOW), DATA, axis=0, tiled=True)
    w_up = lax.all_gather(arrived[:, :, att_columns:], DATA, axis=0)
    w_up = w_up.transpose(1, 0, 2, 3).reshape(width, hidden_lanes)
    w_down = lax.all_gather(down_master.astype(LOW), DATA, axis=0, tiled=True)
    cotangents = gather_z(cotangent)

    unit_first, scale_first = normalise(inputs.astype(WIDE))
    normed = (unit_first * vectors[:, 0] + vectors[:, 1]).astype(LOW)
    query_bias = lax.dynamic_slice_in_dim(vectors[:, 2], place * lanes, lanes)
    value_bias = lax.dynamic_slice_in_dim(vectors[:, 3], place * lanes, lanes)
    qkv_bias = jnp.concatenate([query_bias, jnp.zeros((lanes,), WIDE), value_bias])
    qkv_rows = (dot(normed, w_qkv, ((1,), (0,))) + qkv_bias).astype(LOW)
    query_heads = qkv_rows[:, :lanes].reshape(group, heads, HEAD_DIM)
    key_heads = qkv_rows[:, lanes : 2 * lanes].reshape(group, heads, HEAD_DIM)
    value_heads = qkv_rows[:, 2 * lanes :].reshape(group, heads, HEAD_DIM)

    index = jnp.arange(group, dtype=jnp.int32)
    places = (place + index // rows) % RING * rows + index % rows
    first_end = seg_counts[0, 0]
    second_end = first_end + seg_counts[0, 1]
    image = (places >= first_end).astype(jnp.int32) + (places >= second_end).astype(jnp.int32)
    same_image = (image[:, None] == image[None, :])[None]
    score_scale = HEAD_DIM ** (-0.5)
    scores = (
        jnp.einsum("qhd,khd->hqk", query_heads, key_heads, preferred_element_type=WIDE) * score_scale
    )
    scores = jnp.where(same_image, scores, -1e30)
    row_max = jnp.max(scores, -1, keepdims=True)
    exponent = jnp.exp(scores - row_max)
    row_total = jnp.sum(exponent, -1, keepdims=True)
    probs = exponent / row_total
    attended = jnp.einsum("hqk,khd->qhd", probs.astype(LOW), value_heads, preferred_element_type=WIDE)
    attended = attended.reshape(group, lanes).astype(LOW)
    att_out = scatter_z(dot(attended, w_out, ((1,), (0,))))
    middle = tokens.astype(WIDE) + (att_out + vectors[:, 4])

    unit_mid, scale_mid = normalise(middle)
    normed_mid = gather_z((unit_mid * vectors[:, 5] + vectors[:, 6]).astype(LOW))
    up_bias = lax.dynamic_index_in_dim(vectors[:, 7:11], place, 1, keepdims=False)
    pre_act = dot(normed_mid, w_up, ((1,), (0,))) + up_bias
    below = 0.5 * (1.0 + lax.erf(pre_act * (0.5**0.5)))
    hidden = (pre_act * below).astype(LOW)
    slope = below + pre_act * (jnp.exp(-0.5 * pre_act * pre_act) * 0.3989422804014327)

    grad_hidden = dot(cotangents, w_down, ((1,), (1,)))
    grad_pre_wide = grad_hidden * slope
    grad_pre = grad_pre_wide.astype(LOW)
    grad_normed_mid = scatter_z(dot(grad_pre, w_up, ((1,), (1,))))
    ffn_out = scatter_z(dot(hidden, w_down, ((1,), (0,))))
    layer_out = (middle + (ffn_out + vectors[:, 11])).astype(LOW)
    grad_up = dot(normed_mid, grad_pre, ((0,), (0,)))
    grad_down = dot(hidden, cotangents, ((0,), (0,)))

    def scatter_data(grad):
        return lax.psum_scatter(grad, DATA, scatter_dimension=0, tiled=True)

    def by_owner(grad):
        columns = grad.shape[1]
        return (
            grad.reshape(RING, data, own, columns)
            .transpose(1, 0, 2, 3)
            .reshape(data * RING * own, columns)
        )

    up_sum = scatter_data(by_owner(grad_up)).reshape(RING, own, hidden_lanes)
    down_sum = scatter_data(grad_down)

    grad_middle = cotangent.astype(WIDE) + normalise_back(
        grad_normed_mid, unit_mid, scale_mid, vectors[:, 5]
    )
    grad_mid_own = grad_middle.astype(LOW)
    grad_mid_low = gather_z(grad_mid_own)
    grad_out = dot(attended, grad_mid_low, ((0,), (0,)))
    out_sum = scatter_data(grad_out)

    grad_att = dot(grad_mid_low, w_out, ((1,), (1,))).astype(LOW).reshape(group, heads, HEAD_DIM)
    grad_probs = jnp.einsum("qhd,khd->hqk", grad_att, value_heads, preferred_element_type=WIDE)
    row_inner = jnp.sum(probs * grad_probs, -1, keepdims=True)
    grad_scores = (probs * (grad_probs - row_inner)).astype(LOW)
    grad_query = (
        jnp.einsum("hqk,khd->qhd", grad_scores, key_heads, preferred_element_type=WIDE) * score_scale
    )
    grad_key = (
        jnp.einsum("hqk,qhd->khd", grad_scores, query_heads, preferred_element_type=WIDE)
        * score_scale
    )
    grad_value = jnp.einsum("hqk,qhd->khd", probs.astype(LOW), grad_att, preferred_element_type=WIDE)
    grad_qkv = jnp.concatenate(
        [grad.reshape(group, lanes).astype(LOW) for grad in (grad_query, grad_key, grad_value)],
        axis=1,
    )
    grad_qkv_w = dot(normed, grad_qkv, ((0,), (0,)))
    grad_normed_part = dot(grad_qkv, w_qkv, ((1,), (1,)))

    def in_place(values, length):
        return lax.dynamic_update_slice_in_dim(
            jnp.zeros((length,), WIDE), values, place * lanes, 0
        )

    bias_sums = jnp.sum(grad_qkv, axis=0, dtype=WIDE)
    up_column = jnp.sum(grad_pre, axis=0, dtype=WIDE)
    vec_rows = jnp.stack(
        [
            jnp.sum(grad_normed_part * unit_first, axis=0),
            jnp.sum(grad_normed_part, axis=0),
            in_place(bias_sums[:lanes], width),
            in_place(bias_sums[2 * lanes :], width),
            jnp.sum(grad_mid_own, axis=0, dtype=WIDE),
            jnp.sum(grad_normed_mid * unit_mid, axis=0),
            jnp.sum(grad_normed_mid, axis=0),
        ]
        + [jnp.where(place == k, up_column, 0.0) for k in range(RING)]
        + [jnp.sum(cotangent, axis=0, dtype=WIDE)]
    )
    vec_columns = jnp.pad(vec_rows, ((0, VEC_PAD - vec_rows.shape[0]), (0, 0))).T
    att_sum = scatter_data(by_owner(jnp.concatenate([grad_qkv_w, vec_columns], axis=1)))
    att_sum = att_sum.reshape(RING, own, att_columns)

    grad_normed = scatter_z(grad_normed_part)
    input_grad = (
        grad_middle
        + normalise_back(grad_normed, unit_first[:rows], scale_first[:rows], vectors[:, 0])
    ).astype(LOW)

    home = swap_z(jnp.concatenate([att_sum, up_sum], axis=2))
    qkv_sum = (
        home[:, :, : 3 * lanes]
        .reshape(RING, own, 3, lanes)
        .transpose(1, 2, 0, 3)
        .reshape(own, 3 * width)
    )
    vec_sum = jnp.sum(home[:, :, 3 * lanes : 3 * lanes + vec_master.shape[1]], axis=0)
    up_sum = home[:, :, att_columns:].transpose(1, 0, 2).reshape(own, RING * hidden_lanes)

    firsts = (qkv_first, out_first, up_first, down_first)
    seconds = (qkv_second, out_second, up_second, down_second)
    results = [
        adam_step(grad_sum / data, moment, square, weight, DECAY)
        for grad_sum, moment, square, weight in zip(
            (qkv_sum, out_sum, up_sum, down_sum), firsts, seconds, masters
        )
    ]
    squares = jnp.stack(
        [jnp.sum(matrix * matrix) for matrix in masters]
        + [jnp.sum(parts[2] * parts[2]) for parts in results]
    )
    tile = jnp.broadcast_to(squares[:, None], (8, 128))
    totals = jnp.sqrt(sum_everywhere(tile)[:, 0])
    weight_norm = totals[:4]
    update_norm = totals[4:]
    ratio = weight_norm / update_norm
    new_mats = [
        weight - RATE * ratio[k] * parts[2] for k, (weight, parts) in enumerate(zip(masters, results))
    ]
    vec_moment, vec_square, vec_dir = adam_step(
        vec_sum / data, vec_first, vec_second, vec_master, 0.0
    )
    vec_new = vec_master - VEC_RATE * vec_dir
    matrix_norms = jnp.stack([weight_norm, update_norm], axis=1)
    return (
        layer_out,
        input_grad,
        *new_mats,
        *(parts[0] for parts in results),
        *(parts[1] for parts in results),
        vec_new,
        vec_moment,
        vec_square,
        matrix_norms,
    )


def solution(mesh):
    sizes = (4, 4, 2, 4)
    physical = Mesh(mesh.devices.reshape(sizes), EVERY)
    patches = P(EVERY, None)
    shards = P(("z", *DATA), None)
    return jax.shard_map(
        on_device,
        mesh=physical,
        in_specs=(patches, patches, P(DATA, None)) + (shards,) * 15,
        out_specs=(patches, patches) + (shards,) * 15 + (P(),),
        check_vma=False,
    )
```

time: 1530 us -> 682 us (0.45)
  waiting for transfers between devices: 1060 us -> 359 us
  blocking collectives: 255 us -> 25.1 us
  starting transfers between devices: 1.52 us -> 79.4 us
  matrix products: 114 us -> 84.2 us
  local copies, waits for them, and re-layouts: 28.2 us -> 55.6 us
    reduce_scatter x11 -> x4, waiting for transfers between devices: 697 us -> 228 us  [scatter_data(): return lax.psum_scatter(grad, DATA, scatter_dimension=0, tiled=True)]
    all_gather x9 -> x3, waiting for transfers between devices: 365 us -> 43.6 us  [the longest x1 43.5 us: on_device(): w_down = lax.all_gather(down_master.astype(LOW), DATA, axis=0, tiled=True)]
    unnamed x1 -> x0, blocking collectives: 126 us -> none
    ppermute x0 -> x45, waiting for transfers between devices: none -> 86.6 us  [the longest x38 71.5 us: send(): lax.ppermute(block, axis, [(i, (i + step) % size) for i in range(size)])]
    ppermute x0 -> x45, starting transfers between devices: none -> 78.5 us  [the longest x38 66.6 us: send(): lax.ppermute(block, axis, [(i, (i + step) % size) for i in range(size)])]
    psum x1 -> x0, blocking collectives: 64.8 us -> none  [on_device(): lax.psum((jnp.stack([jnp.sum(matrix * matrix) for matrix in masters]), up...]
    dot_general x15 -> x14, matrix products: 93.3 us -> 53.2 us  [the longest x12 41 us: dot(): lax.dot_general(left, right, (dims, ((), ())), preferred_element_type=WIDE)]
    all_gather x3 -> x1, blocking collectives: 64.2 us -> 25.1 us  [on_device(): w_out = lax.all_gather(out_master.astype(LOW), DATA, axis=0, tiled=True)]
  transfers between devices with their start and end apart: 20 -> 52, of which waited for: 19 -> 30; matrix products, arithmetic and copies ran while one was open for 9% -> 22% of each run, Pallas kernels for 0% -> 0%
where the time goes in v1:
time: 682 us; the launch traced here: 676 us
  waiting for transfers between devices  359 us (53%)
  matrix products  84.2 us (12%)
  starting transfers between devices  79.4 us (12%)
  local copies, waits for them, and re-layouts  55.6 us (8%)
  other arithmetic  52.8 us (8%)
  blocking collectives  25.1 us (4%)
  between operations  19.9 us (3%)
    reduce_scatter x4, waiting for transfers between devices, scatter_data(): return lax.psum_scatter(grad, DATA, scatter_dimension=0, tiled=True)  228 us
    ppermute x38, waiting for transfers between devices, send(): lax.ppermute(block, axis, [(i, (i + step) % size) for i in range(size)])  71.5 us
    ppermute x38, starting transfers between devices, send(): lax.ppermute(block, axis, [(i, (i + step) % size) for i in range(size)])  66.6 us
    all_gather x1, waiting for transfers between devices, on_device(): w_down = lax.all_gather(down_master.astype(LOW), DATA, axis=0, tiled=True)  43.5 us
    dot_general x12, matrix products, dot(): lax.dot_general(left, right, (dims, ((), ())), preferred_element_type=WIDE)  41 us
    all_gather x1, blocking collectives, on_device(): w_out = lax.all_gather(out_master.astype(LOW), DATA, axis=0, tiled=True)  25.1 us
    unnamed x194, local copies, waits for them, and re-layouts  18.2 us
    dot_general x1, matrix products, on_device(): jnp.einsum('qhd,khd->hqk', grad_att, value_heads, preferred_element_type=...  15.6 us
  transfers between devices with their start and end apart: 52, of which 30 were waited for; matrix products, arithmetic and copies ran while one was open for 22% of the time, Pallas kernels for 0%

profile of v1, /device:TPU:0, one launch (start us, length us, event | category | flops | bytes accessed | tf_op | source)
XLA Modules:
  0.0 675.8 jit_solution(16014930564556160612)
XLA Ops:
  9.9 4.2 collective-permute-start.4
  16.0 3.6 collective-permute-done.5
  20.4 3.3 collective-permute-start
  27.1 25.1 %all_gather.20 = bf16[256,1024]{1,0:T(8,128)(2,1)S(1)} all-gather(bf16[8,1024]{1,0:T(8,128)(2,1)S(1)} %convert_element_type.207), channel_id=1, replica_groups=mesh['x'=4,'y'=4,'c'=2,'z'=4] {'x','y','c'}, dimensions={0}, use_global_device_ids=true | all-gather | bytes 540672 | tf_op jit(solution)/shard_map/all_gather | solution.py:155
  57.2 3.3 collective-permute-start.3
  75.2 11.2 %fusion.89 = (f32[4,1024]{1,0:T(4,128)S(1)}, f32[4,1024,1024]{1,2,0:T(8,128)}) fusion(pred[1024,1024]{0,1:T(8,128)(4,1)} %broadcast_compare_fusion, bf16[1024,4,64]{0,2,1:T(8,128)(2,1)S(1)} %bitcast.165, bf16[1024,4,64]{0,2,1:T(8,128)(2,1)S(1)} %bitcast.163), kind=kOutput, calls=%fused_computation.251 | convolution fusion | flops 553649152 | bytes 18890752 | tf_op jit(solution)/shard_map/sub | solution.py:183
  86.4 7.4 %fusion.23 = bf16[4,64,1024]{2,1,0:T(8,128)(2,1)S(1)} fusion(bf16[1024,4,64]{0,2,1:T(8,128)(2,1)S(1)} %bitcast.175, f32[4,1024,1024]{1,2,0:T(8,128)} %get-tuple-element.128, f32[4,1024]{1,0:T(4,128)S(1)} %get-tuple-element.127), kind=kOutput, calls=%fused_computation.44 | convolution fusion | flops 545521664 | bytes 17842176 | tf_op jit(solution)/shard_map/hqk,khd->qhd/dot_general | solution.py:186
  98.5 5.9 collective-permute-done.7
  104.7 3.1 collective-permute-start.10
  108.3 3.2 collective-permute-start.19
  111.6 8.6 %collective-permute-done.10 = bf16[256,1024]{1,0:T(8,128)(2,1)S(1)} collective-permute-done((bf16[256,1024]{1,0:T(8,128)(2,1)S(1)}, bf16[256,1024]{1,0:T(8,128)(2,1)S(1)}, u32[]{:S(2)}, u32[]{:S(2)}) %collective-permute-start.10) | collective-permute-done | bytes 524320 | tf_op jit(solution)/shard_map/ppermute | solution.py:28
  120.1 4.3 collective-permute-done.8
  126.3 3.2 collective-permute-start.11
  129.5 6.1 collective-permute-done.20
  137.4 3.1 collective-permute-start.22
  143.3 6.5 collective-permute-done.21
  154.7 3.2 collective-permute-start.14
  164.1 4.3 multiply_convert_fusion.1
  169.7 4.4 fusion.95
  174.2 80.9 %reduce-scatter.11.cloned.1.call-done = f32[32,1024]{1,0:T(8,128)} async-done(((f32[1024,1024]{1,0:T(8,128)}), f32[32,1024]{1,0:T(8,128)}) %reduce-scatter.11.cloned.1.call-update) | async-done | bytes 131088 | tf_op jit(solution)/shard_map/reduce_scatter | solution.py:209
  257.7 43.5 %all-gather.6.cloned.1.call-done = bf16[1024,1024]{1,0:T(8,128)(2,1)} async-done(((bf16[32,1024]{1,0:T(8,128)(2,1)}), bf16[1024,1024]{1,0:T(8,128)(2,1)}) %all-gather.6.cloned.1.call-update) | async-done | bytes 2097168 | tf_op jit(solution)/shard_map/all_gather | solution.py:158
  301.2 6.6 convert_reduce_fusion.1
  313.7 4.3 fusion.92
  319.2 2.9 collective-permute-start.17
  330.7 3.8 collective-permute-start.18
  334.6 5.8 collective-permute-done.26
  344.1 5.9 collective-permute-done.18
  350.8 3.9 convert_reduce_fusion.4
  362.7 5.6 collective-permute-done.28
  369.0 3.3 collective-permute-start.30
  372.4 3.6 collective-permute-done.29
  378.6 15.6 %multiply_reduce_fusion = (f32[4,1024]{1,0:T(4,128)S(1)}, f32[4,1024,1024]{1,2,0:T(8,128)}) fusion(f32[4,1024,1024]{1,2,0:T(8,128)} %get-tuple-element.128, f32[4,1024]{1,0:T(4,128)S(1)} %get-tuple-element.127, bf16[1024,4,64]{0,2,1:T(8,128)(2,1)S(1)} %bitcast.198, bf16[1024,4,64]{0,2,1:T(8,128)(2,1)S(1)} %bitcast.176), kind=kOutput, calls=%fused_computation.2 | convolution fusion | flops 549449728 | bytes 34635776 | tf_op jit(solution)/shard_map/qhd,khd->hqk/dot_general | solution.py:231
  395.9 7.9 %multiply_convert_fusion = bf16[4,1024,1024]{1,2,0:T(8,128)(2,1)S(1)} fusion(f32[4,1024,1024]{1,2,0:T(8,128)} %get-tuple-element.138, f32[4,1024]{1,0:T(4,128)S(1)} %get-tuple-element.137, f32[4,1024,1024]{1,2,0:T(8,128)S(1)} %bitcast.144, f32[4,1024]{1,0:T(4,128)S(1)} %get-tuple-element.127), kind=kLoop, calls=%fused_computation.1 | loop fusion | flops 16777216 | bytes 41975808 | tf_op jit(solution)/shard_map/convert_element_type | solution.py:233
  408.1 4.8 fusion.26
  414.5 8.0 %fusion.73 = (f32[1024]{0:T(1024)S(1)}, f32[1024]{0:T(1024)S(1)}, bf16[1024,1024]{1,0:T(8,128)(2,1)}, f32[1024,1024]{1,0:T(8,128)}, f32[1024,1024]{1,0:T(8,128)}) fusion(f32[1024]{0:T(1024)S(1)} %copy-done.68, f32[1024]{0:T(1024)S(1)} %copy-done.58, bf16[1024,1024]{1,0:T(8,128)(2,1)S(1)} %copy-done.2, bf16[1024,896]{1,0:T(8,128)(2,1)} %bitcast.151, ...), kind=kOutput, calls=%fused_computation.238 | convolution fusion | flops 1622669312 | bytes 15745024 | tf_op jit(solution)/shard_map/dot_general | solution.py:103
  422.8 3.2 fusion.41
  428.3 5.0 copy.72
  433.3 4.4 copy.73
  442.9 3.3 collective-permute-start.33
  446.2 4.3 collective-permute-done.31
  452.0 3.4 collective-permute-start.34
  455.5 70.8 %reduce-scatter.5.cloned.1.call-done = f32[32,896]{1,0:T(8,128)} async-done(((f32[1024,896]{1,0:T(8,128)}), f32[32,896]{1,0:T(8,128)}) %reduce-scatter.5.cloned.1.call-update) | async-done | bytes 114704 | tf_op jit(solution)/shard_map/reduce_scatter | solution.py:209
  527.2 3.0 collective-permute-start.35
  530.2 76.8 %reduce-scatter.9.cloned.1.call-done = f32[8,1024]{1,0:T(8,128)} async-done(((f32[256,1024]{1,0:T(8,128)}), f32[8,1024]{1,0:T(8,128)}) %reduce-scatter.9.cloned.1.call-update) | async-done | bytes 32784 | tf_op jit(solution)/shard_map/reduce_scatter | solution.py:209
  621.6 5.3 stack.114
  630.7 3.4 collective-permute-done.39
  642.1 3.1 collective-permute-done.41
  647.9 3.1 collective-permute-done.42
  (392 shorter events, 146.6 us)
Async XLA Ops:
  7.2 61.7 %all-gather.8.cloned.1.call-start = ((), (), s32[]{:S(2)}) async-start(), calls=%async_computation.9 | async-start | bytes 1892352 | tf_op jit(solution)/shard_map/all_gather | solution.py:149
  9.9 6.1 collective-permute-start.4
  14.1 5.4 collective-permute-start.6
  14.1 5.4 collective-permute-start.5
  20.4 139.0 %all-gather.10.cloned.1.call-start = ((), (), s32[]{:S(2)}) async-start(), calls=%async_computation.10 | async-start | bytes 2162688 | tf_op jit(solution)/shard_map/all_gather | solution.py:156
  20.4 35.0 %collective-permute-start = (bf16[256,1024]{1,0:T(8,128)(2,1)}, bf16[256,1024]{1,0:T(8,128)(2,1)}, u32[]{:S(2)}, u32[]{:S(2)}) collective-permute-start(bf16[256,1024]{1,0:T(8,128)(2,1)} %param.18), channel_id=1, source_target_pairs={{0,3},{1,0},{2,1},{3,2},{4,7},{5,4},{6,5},{7,6},{8,11},{9,8},{10,9... | collective-permute-start | bytes 1572872 | tf_op jit(solution)/shard_map/ppermute | solution.py:28
  23.7 30.8 %collective-permute-start.1 = (bf16[256,1024]{1,0:T(8,128)(2,1)}, bf16[256,1024]{1,0:T(8,128)(2,1)S(1)}, u32[]{:S(2)}, u32[]{:S(2)}) collective-permute-start(bf16[256,1024]{1,0:T(8,128)(2,1)} %param.18), channel_id=1, source_target_pairs={{0,1},{1,2},{2,3},{3,0},{4,5},{5,6},{6,7},{7,4},{8,9},{9,10},{10,1... | collective-permute-start | bytes 1572872 | tf_op jit(solution)/shard_map/ppermute | solution.py:28
  55.4 10.2 %collective-permute-start.2 = (bf16[128,1024]{1,0:T(8,128)(2,1)}, bf16[128,1024]{1,0:T(8,128)(2,1)S(1)}, u32[]{:S(2)}, u32[]{:S(2)}) collective-permute-start(bf16[128,1024]{1,0:T(8,128)(2,1)} %slice.329), channel_id=1, source_target_pairs={{0,1},{1,2},{2,3},{3,0},{4,5},{5,6},{6,7},{7,4},{8,9},{9,10},{10,1... | collective-permute-start | bytes 786440 | tf_op jit(solution)/shard_map/ppermute | solution.py:28
  57.2 9.6 %collective-permute-start.3 = (bf16[128,1024]{1,0:T(8,128)(2,1)}, bf16[128,1024]{1,0:T(8,128)(2,1)}, u32[]{:S(2)}, u32[]{:S(2)}) collective-permute-start(bf16[128,1024]{1,0:T(8,128)(2,1)} %slice.330), channel_id=1, source_target_pairs={{0,3},{1,0},{2,1},{3,2},{4,7},{5,4},{6,5},{7,6},{8,11},{9,8},{10,9... | collective-permute-start | bytes 786440 | tf_op jit(solution)/shard_map/ppermute | solution.py:28
  61.9 193.2 %reduce-scatter.11.cloned.1.call-start = ((), (), s32[]{:S(2)}) async-start(), calls=%async_computation.8 | async-start | bytes 4325376 | tf_op jit(solution)/shard_map/reduce_scatter | solution.py:209
  94.7 9.7 %collective-permute-start.7 = (bf16[128,1024]{1,0:T(8,128)(2,1)S(1)}, bf16[128,1024]{1,0:T(8,128)(2,1)S(1)}, u32[]{:S(2)}, u32[]{:S(2)}) collective-permute-start(bf16[128,1024]{1,0:T(8,128)(2,1)S(1)} %get-tuple-element.82), channel_id=1, source_target_pairs={{0,1},{1,2},{2,3},{3,0},{4,5},{5,6},{6,7},{7,4},{8,9},{9,10},{10,1... | collective-permute-start | bytes 786440 | tf_op jit(solution)/shard_map/ppermute | solution.py:28
  96.6 7.8 %collective-permute-start.9 = (bf16[128,1024]{1,0:T(8,128)(2,1)S(1)}, bf16[128,1024]{1,0:T(8,128)(2,1)S(1)}, u32[]{:S(2)}, u32[]{:S(2)}) collective-permute-start(bf16[128,1024]{1,0:T(8,128)(2,1)S(1)} %get-tuple-element.83), channel_id=1, source_target_pairs={{0,3},{1,0},{2,1},{3,2},{4,7},{5,4},{6,5},{7,6},{8,11},{9,8},{10,9... | collective-permute-start | bytes 786440 | tf_op jit(solution)/shard_map/ppermute | solution.py:28
  104.7 15.5 %collective-permute-start.10 = (bf16[256,1024]{1,0:T(8,128)(2,1)S(1)}, bf16[256,1024]{1,0:T(8,128)(2,1)S(1)}, u32[]{:S(2)}, u32[]{:S(2)}) collective-permute-start(bf16[256,1024]{1,0:T(8,128)(2,1)S(1)} %pad_maximum_fusion.3), channel_id=1, source_target_pairs={{0,3},{1,0},{2,1},{3,2},{4,7},{5,4},{6,5},{7,6},{8,11},{9,8},{10,9... | collective-permute-start | bytes 1572872 | tf_op jit(solution)/shard_map/ppermute | solution.py:28
  107.8 16.6 %collective-permute-start.8 = (bf16[256,1024]{1,0:T(8,128)(2,1)S(1)}, bf16[256,1024]{1,0:T(8,128)(2,1)S(1)}, u32[]{:S(2)}, u32[]{:S(2)}) collective-permute-start(bf16[256,1024]{1,0:T(8,128)(2,1)S(1)} %pad_maximum_fusion.2), channel_id=1, source_target_pairs={{0,1},{1,2},{2,3},{3,0},{4,5},{5,6},{6,7},{7,4},{8,9},{9,10},{10,1... | collective-permute-start | bytes 1572872 | tf_op jit(solution)/shard_map/ppermute | solution.py:28
  108.3 28.1 %collective-permute-start.19 = (bf16[256,1024]{1,0:T(8,128)(2,1)S(1)}, bf16[256,1024]{1,0:T(8,128)(2,1)S(1)}, u32[]{:S(2)}, u32[]{:S(2)}) collective-permute-start(bf16[256,1024]{1,0:T(8,128)(2,1)S(1)} %copy-done.11), channel_id=1, source_target_pairs={{0,3},{1,0},{2,1},{3,2},{4,7},{5,4},{6,5},{7,6},{8,11},{9,8},{10,9... | collective-permute-start | bytes 1572872 | tf_op jit(solution)/shard_map/ppermute | solution.py:28
  111.6 24.1 %collective-permute-start.20 = (bf16[256,1024]{1,0:T(8,128)(2,1)S(1)}, bf16[256,1024]{1,0:T(8,128)(2,1)S(1)}, u32[]{:S(2)}, u32[]{:S(2)}) collective-permute-start(bf16[256,1024]{1,0:T(8,128)(2,1)S(1)} %copy-done.11), channel_id=1, source_target_pairs={{0,1},{1,2},{2,3},{3,0},{4,5},{5,6},{6,7},{7,4},{8,9},{9,10},{10,1... | collective-permute-start | bytes 1572872 | tf_op jit(solution)/shard_map/ppermute | solution.py:28
  126.3 24.2 %collective-permute-start.12 = (bf16[256,1024]{1,0:T(8,128)(2,1)}, bf16[256,1024]{1,0:T(8,128)(2,1)S(1)}, u32[]{:S(2)}, u32[]{:S(2)}) collective-permute-start(bf16[256,1024]{1,0:T(8,128)(2,1)} %get-tuple-element.57), channel_id=1, source_target_pairs={{0,1},{1,2},{2,3},{3,0},{4,5},{5,6},{6,7},{7,4},{8,9},{9,10},{10,1... | collective-permute-start | bytes 1572872 | tf_op jit(solution)/shard_map/ppermute | solution.py:28
  126.3 26.7 %collective-permute-start.11 = (bf16[256,1024]{1,0:T(8,128)(2,1)}, bf16[256,1024]{1,0:T(8,128)(2,1)}, u32[]{:S(2)}, u32[]{:S(2)}) collective-permute-start(bf16[256,1024]{1,0:T(8,128)(2,1)} %get-tuple-element.57), channel_id=1, source_target_pairs={{0,3},{1,0},{2,1},{3,2},{4,7},{5,4},{6,5},{7,6},{8,11},{9,8},{10,9... | collective-permute-start | bytes 1572872 | tf_op jit(solution)/shard_map/ppermute | solution.py:28
  136.4 13.4 %collective-permute-start.21 = (bf16[128,1024]{1,0:T(8,128)(2,1)}, bf16[128,1024]{1,0:T(8,128)(2,1)S(1)}, u32[]{:S(2)}, u32[]{:S(2)}) collective-permute-start(bf16[128,1024]{1,0:T(8,128)(2,1)} %slice.361), channel_id=1, source_target_pairs={{0,1},{1,2},{2,3},{3,0},{4,5},{5,6},{6,7},{7,4},{8,9},{9,10},{10,1... | collective-permute-start | bytes 786440 | tf_op jit(solution)/shard_map/ppermute | solution.py:28
  137.4 13.9 %collective-permute-start.22 = (bf16[128,1024]{1,0:T(8,128)(2,1)}, bf16[128,1024]{1,0:T(8,128)(2,1)}, u32[]{:S(2)}, u32[]{:S(2)}) collective-permute-start(bf16[128,1024]{1,0:T(8,128)(2,1)} %slice.362), channel_id=1, source_target_pairs={{0,3},{1,0},{2,1},{3,2},{4,7},{5,4},{6,5},{7,6},{8,11},{9,8},{10,9... | collective-permute-start | bytes 786440 | tf_op jit(solution)/shard_map/ppermute | solution.py:28
  151.3 11.8 %collective-permute-start.13 = (bf16[128,1024]{1,0:T(8,128)(2,1)}, bf16[128,1024]{1,0:T(8,128)(2,1)S(1)}, u32[]{:S(2)}, u32[]{:S(2)}) collective-permute-start(bf16[128,1024]{1,0:T(8,128)(2,1)} %slice.350), channel_id=1, source_target_pairs={{0,1},{1,2},{2,3},{3,0},{4,5},{5,6},{6,7},{7,4},{8,9},{9,10},{10,1... | collective-permute-start | bytes 786440 | tf_op jit(solution)/shard_map/ppermute | solution.py:28
  154.7 8.4 %collective-permute-start.14 = (bf16[128,1024]{1,0:T(8,128)(2,1)}, bf16[128,1024]{1,0:T(8,128)(2,1)}, u32[]{:S(2)}, u32[]{:S(2)}) collective-permute-start(bf16[128,1024]{1,0:T(8,128)(2,1)} %slice.351), channel_id=1, source_target_pairs={{0,3},{1,0},{2,1},{3,2},{4,7},{5,4},{6,5},{7,6},{8,11},{9,8},{10,9... | collective-permute-start | bytes 786440 | tf_op jit(solution)/shard_map/ppermute | solution.py:28
  174.2 127.0 %all-gather.6.cloned.1.call-start = ((), (), s32[]{:S(2)}) async-start(), calls=%async_computation.4 | async-start | bytes 2162688 | tf_op jit(solution)/shard_map/all_gather | solution.py:158
  257.4 198.1 %reduce-scatter.7.cloned.1.call-start = ((), (), s32[]{:S(2)}) async-start(), calls=%async_computation.6 | async-start | bytes 4325376 | tf_op jit(solution)/shard_map/reduce_scatter | solution.py:209
  310.4 11.8 %collective-permute-start.23 = (bf16[128,1024]{1,0:T(8,128)(2,1)S(1)}, bf16[128,1024]{1,0:T(8,128)(2,1)S(1)}, u32[]{:S(2)}, u32[]{:S(2)}) collective-permute-start(bf16[128,1024]{1,0:T(8,128)(2,1)S(1)} %get-tuple-element.74), channel_id=1, source_target_pairs={{0,1},{1,2},{2,3},{3,0},{4,5},{5,6},{6,7},{7,4},{8,9},{9,10},{10,1... | collective-permute-start | bytes 786440 | tf_op jit(solution)/shard_map/ppermute | solution.py:28
  312.0 10.1 %collective-permute-start.25 = (bf16[128,1024]{1,0:T(8,128)(2,1)S(1)}, bf16[128,1024]{1,0:T(8,128)(2,1)S(1)}, u32[]{:S(2)}, u32[]{:S(2)}) collective-permute-start(bf16[128,1024]{1,0:T(8,128)(2,1)S(1)} %get-tuple-element.75), channel_id=1, source_target_pairs={{0,3},{1,0},{2,1},{3,2},{4,7},{5,4},{6,5},{7,6},{8,11},{9,8},{10,9... | collective-permute-start | bytes 786440 | tf_op jit(solution)/shard_map/ppermute | solution.py:28
  318.9 9.8 %collective-permute-start.15 = (bf16[128,1024]{1,0:T(8,128)(2,1)}, bf16[128,1024]{1,0:T(8,128)(2,1)}, u32[]{:S(2)}, u32[]{:S(2)}) collective-permute-start(bf16[128,1024]{1,0:T(8,128)(2,1)} %get-tuple-element.78), channel_id=1, source_target_pairs={{0,1},{1,2},{2,3},{3,0},{4,5},{5,6},{6,7},{7,4},{8,9},{9,10},{10,1... | collective-permute-start | bytes 786440 | tf_op jit(solution)/shard_map/ppermute | solution.py:28
  319.2 10.0 %collective-permute-start.17 = (bf16[128,1024]{1,0:T(8,128)(2,1)}, bf16[128,1024]{1,0:T(8,128)(2,1)}, u32[]{:S(2)}, u32[]{:S(2)}) collective-permute-start(bf16[128,1024]{1,0:T(8,128)(2,1)} %get-tuple-element.79), channel_id=1, source_target_pairs={{0,3},{1,0},{2,1},{3,2},{4,7},{5,4},{6,5},{7,6},{8,11},{9,8},{10,9... | collective-permute-start | bytes 786440 | tf_op jit(solution)/shard_map/ppermute | solution.py:28
  323.1 17.3 %collective-permute-start.26 = (bf16[256,1024]{1,0:T(8,128)(2,1)}, bf16[256,1024]{1,0:T(8,128)(2,1)}, u32[]{:S(2)}, u32[]{:S(2)}) collective-permute-start(bf16[256,1024]{1,0:T(8,128)(2,1)} %pad_maximum_fusion.7), channel_id=1, source_target_pairs={{0,3},{1,0},{2,1},{3,2},{4,7},{5,4},{6,5},{7,6},{8,11},{9,8},{10,9... | collective-permute-start | bytes 1572872 | tf_op jit(solution)/shard_map/ppermute | solution.py:28
  325.0 16.4 %collective-permute-start.24 = (bf16[256,1024]{1,0:T(8,128)(2,1)}, bf16[256,1024]{1,0:T(8,128)(2,1)}, u32[]{:S(2)}, u32[]{:S(2)}) collective-permute-start(bf16[256,1024]{1,0:T(8,128)(2,1)} %pad_maximum_fusion.6), channel_id=1, source_target_pairs={{0,1},{1,2},{2,3},{3,0},{4,5},{5,6},{6,7},{7,4},{8,9},{9,10},{10,1... | collective-permute-start | bytes 1572872 | tf_op jit(solution)/shard_map/ppermute | solution.py:28
  330.7 19.3 %collective-permute-start.18 = (bf16[256,1024]{1,0:T(8,128)(2,1)S(1)}, bf16[256,1024]{1,0:T(8,128)(2,1)S(1)}, u32[]{:S(2)}, u32[]{:S(2)}) collective-permute-start(bf16[256,1024]{1,0:T(8,128)(2,1)S(1)} %pad_maximum_fusion.5), channel_id=1, source_target_pairs={{0,3},{1,0},{2,1},{3,2},{4,7},{5,4},{6,5},{7,6},{8,11},{9,8},{10,9... | collective-permute-start | bytes 1572872 | tf_op jit(solution)/shard_map/ppermute | solution.py:28
  334.5 16.2 %collective-permute-start.16 = (bf16[256,1024]{1,0:T(8,128)(2,1)S(1)}, bf16[256,1024]{1,0:T(8,128)(2,1)S(1)}, u32[]{:S(2)}, u32[]{:S(2)}) collective-permute-start(bf16[256,1024]{1,0:T(8,128)(2,1)S(1)} %pad_maximum_fusion.4), channel_id=1, source_target_pairs={{0,1},{1,2},{2,3},{3,0},{4,5},{5,6},{6,7},{7,4},{8,9},{9,10},{10,1... | collective-permute-start | bytes 1572872 | tf_op jit(solution)/shard_map/ppermute | solution.py:28
  354.6 13.6 %collective-permute-start.28 = (bf16[256,1024]{1,0:T(8,128)(2,1)S(1)}, bf16[256,1024]{1,0:T(8,128)(2,1)S(1)}, u32[]{:S(2)}, u32[]{:S(2)}) collective-permute-start(bf16[256,1024]{1,0:T(8,128)(2,1)S(1)} %get-tuple-element.52), channel_id=1, source_target_pairs={{0,1},{1,2},{2,3},{3,0},{4,5},{5,6},{6,7},{7,4},{8,9},{9,10},{10,1... | collective-permute-start | bytes 1572872 | tf_op jit(solution)/shard_map/ppermute | solution.py:28
  355.0 14.0 %collective-permute-start.27 = (bf16[256,1024]{1,0:T(8,128)(2,1)S(1)}, bf16[256,1024]{1,0:T(8,128)(2,1)S(1)}, u32[]{:S(2)}, u32[]{:S(2)}) collective-permute-start(bf16[256,1024]{1,0:T(8,128)(2,1)S(1)} %get-tuple-element.52), channel_id=1, source_target_pairs={{0,3},{1,0},{2,1},{3,2},{4,7},{5,4},{6,5},{7,6},{8,11},{9,8},{10,9... | collective-permute-start | bytes 1572872 | tf_op jit(solution)/shard_map/ppermute | solution.py:28
  362.6 163.6 %reduce-scatter.5.cloned.1.call-start = ((), (), s32[]{:S(2)}) async-start(), calls=%async_computation.5 | async-start | bytes 3784704 | tf_op jit(solution)/shard_map/reduce_scatter | solution.py:209
  368.3 7.7 %collective-permute-start.29 = (bf16[128,1024]{1,0:T(8,128)(2,1)S(1)}, bf16[128,1024]{1,0:T(8,128)(2,1)S(1)}, u32[]{:S(2)}, u32[]{:S(2)}) collective-permute-start(bf16[128,1024]{1,0:T(8,128)(2,1)S(1)} %slice.370), channel_id=1, source_target_pairs={{0,1},{1,2},{2,3},{3,0},{4,5},{5,6},{6,7},{7,4},{8,9},{9,10},{10,1... | collective-permute-start | bytes 786440 | tf_op jit(solution)/shard_map/ppermute | solution.py:28
  369.0 7.2 %collective-permute-start.30 = (bf16[128,1024]{1,0:T(8,128)(2,1)S(1)}, bf16[128,1024]{1,0:T(8,128)(2,1)S(1)}, u32[]{:S(2)}, u32[]{:S(2)}) collective-permute-start(bf16[128,1024]{1,0:T(8,128)(2,1)S(1)} %slice.371), channel_id=1, source_target_pairs={{0,3},{1,0},{2,1},{3,2},{4,7},{5,4},{6,5},{7,6},{8,11},{9,8},{10,9... | collective-permute-start | bytes 786440 | tf_op jit(solution)/shard_map/ppermute | solution.py:28
  437.7 169.2 %reduce-scatter.9.cloned.1.call-start = ((), (), s32[]{:S(2)}) async-start(), calls=%async_computation.7 | async-start | bytes 1081344 | tf_op jit(solution)/shard_map/reduce_scatter | solution.py:209
  442.4 8.1 %collective-permute-start.31 = (bf16[128,1024]{1,0:T(8,128)(2,1)S(1)}, bf16[128,1024]{1,0:T(8,128)(2,1)S(1)}, u32[]{:S(2)}, u32[]{:S(2)}) collective-permute-start(bf16[128,1024]{1,0:T(8,128)(2,1)S(1)} %get-tuple-element.70), channel_id=1, source_target_pairs={{0,1},{1,2},{2,3},{3,0},{4,5},{5,6},{6,7},{7,4},{8,9},{9,10},{10,1... | collective-permute-start | bytes 786440 | tf_op jit(solution)/shard_map/ppermute | solution.py:28
  442.9 7.6 %collective-permute-start.33 = (bf16[128,1024]{1,0:T(8,128)(2,1)S(1)}, bf16[128,1024]{1,0:T(8,128)(2,1)S(1)}, u32[]{:S(2)}, u32[]{:S(2)}) collective-permute-start(bf16[128,1024]{1,0:T(8,128)(2,1)S(1)} %get-tuple-element.71), channel_id=1, source_target_pairs={{0,3},{1,0},{2,1},{3,2},{4,7},{5,4},{6,5},{7,6},{8,11},{9,8},{10,9... | collective-permute-start | bytes 786440 | tf_op jit(solution)/shard_map/ppermute | solution.py:28
  452.0 185.7 %collective-permute-start.34 = (bf16[256,1024]{1,0:T(8,128)(2,1)S(1)}, bf16[256,1024]{1,0:T(8,128)(2,1)S(1)}, u32[]{:S(2)}, u32[]{:S(2)}) collective-permute-start(bf16[256,1024]{1,0:T(8,128)(2,1)S(1)} %pad_maximum_fusion.9), channel_id=1, source_target_pairs={{0,3},{1,0},{2,1},{3,2},{4,7},{5,4},{6,5},{7,6},{8,11},{9,8},{10,9... | collective-permute-start | bytes 1572872 | tf_op jit(solution)/shard_map/ppermute | solution.py:28
  455.4 182.3 %collective-permute-start.32 = (bf16[256,1024]{1,0:T(8,128)(2,1)S(1)}, bf16[256,1024]{1,0:T(8,128)(2,1)S(1)}, u32[]{:S(2)}, u32[]{:S(2)}) collective-permute-start(bf16[256,1024]{1,0:T(8,128)(2,1)S(1)} %pad_maximum_fusion.8), channel_id=1, source_target_pairs={{0,1},{1,2},{2,3},{3,0},{4,5},{5,6},{6,7},{7,4},{8,9},{9,10},{10,1... | collective-permute-start | bytes 1572872 | tf_op jit(solution)/shard_map/ppermute | solution.py:28
  527.2 86.2 %collective-permute-start.35 = (f32[8,1920]{1,0:T(8,128)S(1)}, f32[8,1920]{1,0:T(8,128)S(1)}, u32[]{:S(2)}, u32[]{:S(2)}) collective-permute-start(f32[8,1920]{1,0:T(8,128)S(1)} %get-tuple-element.105), channel_id=1, source_target_pairs={{0,3},{1,0},{2,1},{3,2},{4,7},{5,4},{6,5},{7,6},{8,11},{9,8},{10,9... | collective-permute-start | bytes 184328 | tf_op jit(solution)/shard_map/ppermute | solution.py:28
  609.0 7.3 %collective-permute-start.37 = (f32[8,1920]{1,0:T(8,128)S(1)}, f32[8,1920]{1,0:T(8,128)S(1)}, u32[]{:S(2)}, u32[]{:S(2)}) collective-permute-start(f32[8,1920]{1,0:T(8,128)S(1)} %get-tuple-element.103), channel_id=1, source_target_pairs={{0,1},{1,2},{2,3},{3,0},{4,5},{5,6},{6,7},{7,4},{8,9},{9,10},{10,1... | collective-permute-start | bytes 184328 | tf_op jit(solution)/shard_map/ppermute | solution.py:28
  610.5 5.7 collective-permute-start.36
  635.0 5.8 collective-permute-start.40
  645.2 5.8 collective-permute-start.42
  656.0 5.8 collective-permute-start.44
  (89 other events, 2306.1 us)
Sparse Core Ops, SparseCore 0:
  20.5 44.9 all-gather.7
  68.3 42.9 all-gather.9
  174.3 80.7 reduce-scatter.10
  258.1 43.0 all-gather.5
  362.8 79.6 reduce-scatter.6
  445.9 80.3 reduce-scatter.4
  530.2 76.7 reduce-scatter.8

commit v2 on v1

--- a/solution.py
+++ b/solution.py
@@ -1,6 +1,8 @@
 import jax
 import jax.numpy as jnp
 from jax import lax
+from jax.experimental import pallas as pl
+from jax.experimental.pallas import tpu as pltpu
 from jax.sharding import Mesh
 from jax.sharding import PartitionSpec as P
 
@@ -60,6 +62,108 @@
 
     arrived = jnp.stack([piece(0), send(piece(3), "z", 3), send(piece(2), "z", 2), send(piece(1), "z", 1)])
     return jnp.roll(arrived, place, axis=0)
+
+
+def send_split(block, phase, step):
+    sizes = [lax.axis_size(axis) for axis in DATA]
+    pairs = []
+    for x in range(sizes[0]):
+        for y in range(sizes[1]):
+            for c in range(sizes[2]):
+                if c == phase:
+                    to = ((x + step) % sizes[0], y)
+                else:
+                    to = (x, (y + step) % sizes[1])
+                pairs.append(
+                    ((x * sizes[1] + y) * sizes[2] + c, (to[0] * sizes[1] + to[1]) * sizes[2] + c)
+                )
+    return lax.ppermute(block, DATA, pairs)
+
+
+def chip_of(where, first, second):
+    x, y, c = where[0], where[1], where[2]
+    along_x = (x + jnp.where(c == 0, first, second)) % RING
+    along_y = (y + jnp.where(c == 0, second, first)) % RING
+    return along_x * RING + along_y
+
+
+def place_kernel(where, pieces, out):
+    for second in range(RING):
+        for first in range(RING):
+            out[:, chip_of(where, first, second)] = pieces[second, first]
+
+
+def place_by_chip(pieces, where):
+    shape = pieces.shape
+    return pl.pallas_call(
+        place_kernel,
+        out_shape=jax.ShapeDtypeStruct((shape[2], RING * RING, *shape[3:]), pieces.dtype),
+        in_specs=[
+            pl.BlockSpec(memory_space=pltpu.SMEM),
+            pl.BlockSpec(memory_space=pltpu.VMEM),
+        ],
+        out_specs=pl.BlockSpec(memory_space=pltpu.VMEM),
+        compiler_params=pltpu.CompilerParams(vmem_limit_bytes=32 << 20),
+    )(where, pieces)
+
+
+def gather_chips(shard, where):
+    core = where[2]
+    other = send(shard, "c", 1)
+    both = jnp.where(
+        core == 0, jnp.concatenate([shard, other], 1), jnp.concatenate([other, shard], 1)
+    )
+    half = both.shape[0] // 2
+    block = lax.dynamic_slice_in_dim(both, core * half, half, 0)
+    for phase in range(2):
+        block = jnp.stack(
+            [block] + [send_split(block, phase, -distance) for distance in range(1, RING)]
+        )
+    mine = place_by_chip(block, where)
+    theirs = send(mine, "c", 1)
+    return jnp.concatenate(
+        [jnp.where(core == 0, mine, theirs), jnp.where(core == 0, theirs, mine)]
+    )
+
+
+def arrange_kernel(where, grad, arrived, own, *gone):
+    for second in range(RING):
+        for first in range(RING):
+            chip = chip_of(where, first, second)
+            total = grad[:, chip] + arrived[:, chip].astype(WIDE)
+            if first == 0:
+                own[second] = total
+            else:
+                gone[first - 1][second] = total.astype(LOW)
+
+
+def scatter_chips(grad, where):
+    depth, chips, rows, columns = grad.shape
+    half = depth // 2
+    core = where[2]
+    arrived = send(lax.dynamic_slice_in_dim(grad, (1 - core) * half, half, 0).astype(LOW), "c", 1)
+    piece = (RING, half, rows, columns)
+    own, *gone = pl.pallas_call(
+        arrange_kernel,
+        out_shape=[jax.ShapeDtypeStruct(piece, WIDE)] + [jax.ShapeDtypeStruct(piece, LOW)] * 3,
+        grid_spec=pltpu.PrefetchScalarGridSpec(
+            num_scalar_prefetch=1,
+            grid=(1,),
+            in_specs=[
+                pl.BlockSpec((half, chips, rows, columns), lambda i, where: (where[2], 0, 0, 0)),
+                pl.BlockSpec((half, chips, rows, columns), lambda i, where: (0, 0, 0, 0)),
+            ],
+            out_specs=[pl.BlockSpec(piece, lambda i, where: (0, 0, 0, 0))] * 4,
+        ),
+        compiler_params=pltpu.CompilerParams(vmem_limit_bytes=48 << 20),
+    )(where, grad, arrived)
+    total = own
+    for distance in range(1, RING):
+        total = total + send_split(gone[distance - 1], 0, distance).astype(WIDE)
+    own, low = total[0], total.astype(LOW)
+    for distance in range(1, RING):
+        own = own + send_split(low[distance], 1, distance).astype(WIDE)
+    return own
 
 
 def sum_everywhere(values):
@@ -125,6 +229,8 @@
 ):
     masters = (qkv_master, out_master, up_master, down_master)
     place = lax.axis_index("z")
+    core = lax.axis_index("c")
+    where = jnp.stack([lax.axis_index(axis) for axis in DATA]).astype(jnp.int32)
     rows, width = tokens.shape
     own = qkv_master.shape[0]
     lanes = width // RING
@@ -144,18 +250,33 @@
     weight_parts = jnp.concatenate(
         [qkv_parts, jnp.broadcast_to(vec_low, (RING, own, VEC_PAD)), up_parts], axis=2
     )
+    inputs = gather_z(tokens)
     arrived = swap_z(weight_parts)
     att_columns = 3 * lanes + VEC_PAD
-    first_pack = lax.all_gather(arrived[:, :, :att_columns], DATA, axis=0)
-    first_pack = first_pack.transpose(1, 0, 2, 3).reshape(width, att_columns)
-    w_qkv = first_pack[:, : 3 * lanes]
-    vectors = first_pack[:, 3 * lanes : 3 * lanes + vec_master.shape[1]].astype(WIDE)
-
-    inputs = gather_z(tokens)
-    w_out = lax.all_gather(out_master.astype(LOW), DATA, axis=0, tiled=True)
-    w_up = lax.all_gather(arrived[:, :, att_columns:], DATA, axis=0)
-    w_up = w_up.transpose(1, 0, 2, 3).reshape(width, hidden_lanes)
-    w_down = lax.all_gather(down_master.astype(LOW), DATA, axis=0, tiled=True)
+    out_parts = out_master.astype(LOW).reshape(own, RING, lanes).transpose(1, 0, 2)
+    att_weights = gather_chips(
+        jnp.concatenate([arrived[:, :, :att_columns], out_parts], axis=2), where
+    )
+    att_rows = att_weights.reshape(width, att_columns + lanes)
+    w_qkv = att_rows[:, : 3 * lanes]
+    vectors = att_rows[:, 3 * lanes : 3 * lanes + vec_master.shape[1]].astype(WIDE)
+    w_out = (
+        att_weights.reshape(RING, lanes, att_columns + lanes)[:, :, att_columns:]
+        .transpose(1, 0, 2)
+        .reshape(lanes, width)
+    )
+
+    ffn_shard = jnp.concatenate(
+        [arrived[:, :, att_columns:].reshape(RING * own, hidden_lanes), down_master.astype(LOW)]
+    )
+    ffn_weights = lax.all_gather(ffn_shard, DATA, axis=0)
+    w_up = (
+        ffn_weights[:, : RING * own]
+        .reshape(data, RING, own, hidden_lanes)
+        .transpose(1, 0, 2, 3)
+        .reshape(width, hidden_lanes)
+    )
+    w_down = ffn_weights[:, RING * own :].reshape(hidden_lanes, width)
     cotangents = gather_z(cotangent)
 
     unit_first, scale_first = normalise(inputs.astype(WIDE))
@@ -205,19 +326,19 @@
     grad_up = dot(normed_mid, grad_pre, ((0,), (0,)))
     grad_down = dot(hidden, cotangents, ((0,), (0,)))
 
-    def scatter_data(grad):
-        return lax.psum_scatter(grad, DATA, scatter_dimension=0, tiled=True)
-
-    def by_owner(grad):
-        columns = grad.shape[1]
-        return (
-            grad.reshape(RING, data, own, columns)
+    ffn_grads = jnp.concatenate(
+        [
+            grad_up.astype(LOW)
+            .reshape(RING, data, own, hidden_lanes)
             .transpose(1, 0, 2, 3)
-            .reshape(data * RING * own, columns)
-        )
-
-    up_sum = scatter_data(by_owner(grad_up)).reshape(RING, own, hidden_lanes)
-    down_sum = scatter_data(grad_down)
+            .reshape(data, RING * own, hidden_lanes),
+            grad_down.astype(LOW).reshape(data, RING * own, width),
+        ],
+        axis=1,
+    )
+    ffn_sum = lax.psum_scatter(ffn_grads, DATA, scatter_dimension=0).astype(WIDE)
+    up_sum = ffn_sum[: RING * own].reshape(RING, own, hidden_lanes)
+    down_sum = ffn_sum[RING * own :]
 
     grad_middle = cotangent.astype(WIDE) + normalise_back(
         grad_normed_mid, unit_mid, scale_mid, vectors[:, 5]
@@ -225,7 +346,6 @@
     grad_mid_own = grad_middle.astype(LOW)
     grad_mid_low = gather_z(grad_mid_own)
     grad_out = dot(attended, grad_mid_low, ((0,), (0,)))
-    out_sum = scatter_data(grad_out)
 
     grad_att = dot(grad_mid_low, w_out, ((1,), (1,))).astype(LOW).reshape(group, heads, HEAD_DIM)
     grad_probs = jnp.einsum("qhd,khd->hqk", grad_att, value_heads, preferred_element_type=WIDE)
@@ -267,8 +387,19 @@
         + [jnp.sum(cotangent, axis=0, dtype=WIDE)]
     )
     vec_columns = jnp.pad(vec_rows, ((0, VEC_PAD - vec_rows.shape[0]), (0, 0))).T
-    att_sum = scatter_data(by_owner(jnp.concatenate([grad_qkv_w, vec_columns], axis=1)))
-    att_sum = att_sum.reshape(RING, own, att_columns)
+    out_blocks = grad_out.reshape(lanes, RING, lanes).transpose(1, 0, 2).reshape(width, lanes)
+    att_grads = jnp.concatenate([grad_qkv_w, vec_columns, out_blocks], axis=1)
+    chips = data // 2
+    att_sum = scatter_chips(
+        att_grads.reshape(RING, chips, 2 * own, att_columns + lanes), where
+    ).reshape(RING // 2, 2, own, att_columns + lanes)
+    kept = lax.dynamic_index_in_dim(att_sum, core, 1, keepdims=False)
+    given = send(lax.dynamic_index_in_dim(att_sum, 1 - core, 1, keepdims=False), "c", 1)
+    att_sum = jnp.concatenate(
+        [jnp.where(core == 0, kept, given), jnp.where(core == 0, given, kept)]
+    )
+    out_sum = att_sum[:, :, att_columns:].transpose(1, 0, 2).reshape(own, width)
+    att_sum = att_sum[:, :, :att_columns]
 
     grad_normed = scatter_z(grad_normed_part)
     input_grad = (

time: 682 us -> 392 us (0.57)
  waiting for transfers between devices: 359 us -> 102 us
  blocking collectives: 25.1 us -> 0 us
  other arithmetic: 52.8 us -> 42.7 us
  starting transfers between devices: 79.4 us -> 89.4 us
    reduce_scatter x4 -> x1, waiting for transfers between devices: 228 us -> 0.01 us  [on_device(): lax.psum_scatter(ffn_grads, DATA, scatter_dimension=0).astype(WIDE)]
    all_gather x3 -> x1, waiting for transfers between devices: 43.6 us -> 0.01 us  [on_device(): ffn_weights = lax.all_gather(ffn_shard, DATA, axis=0)]
    all_gather x1 -> x0, blocking collectives: 25.1 us -> none  [on_device(): w_out = lax.all_gather(out_master.astype(LOW), DATA, axis=0, tiled=True)]
    ppermute x0 -> x12, starting transfers between devices: none -> 23 us  [send_split(): return lax.ppermute(block, DATA, pairs)]
    ppermute x0 -> x12, waiting for transfers between devices: none -> 13.3 us  [send_split(): return lax.ppermute(block, DATA, pairs)]
    transpose x3 -> x2, local copies, waits for them, and re-layouts: 7.94 us -> 0.38 us  [the longest x1 0.21 us: on_device(): ffn_grads = jnp.concatenate([grad_up.astype(LOW).reshape(RING, data, own,...]
    ppermute x38 -> x42, starting transfers between devices: 66.6 us -> 59.2 us  [send(): lax.ppermute(block, axis, [(i, (i + step) % size) for i in range(size)])]
    ppermute x38 -> x42, waiting for transfers between devices: 71.5 us -> 69.3 us  [send(): lax.ppermute(block, axis, [(i, (i + step) % size) for i in range(size)])]
  transfers between devices with their start and end apart: 52 -> 63, of which waited for: 30 -> 36; matrix products, arithmetic and copies ran while one was open for 22% -> 38% of each run, Pallas kernels for 0% -> 1%
where the time goes in v2:
time: 392 us; the launch traced here: 386 us
  waiting for transfers between devices  102 us (26%)
  starting transfers between devices  89.4 us (23%)
  matrix products  79.1 us (20%)
  local copies, waits for them, and re-layouts  49.5 us (13%)
  other arithmetic  42.7 us (11%)
  between operations  19.8 us (5%)
    ppermute x42, waiting for transfers between devices, send(): lax.ppermute(block, axis, [(i, (i + step) % size) for i in range(size)])  69.3 us
    ppermute x42, starting transfers between devices, send(): lax.ppermute(block, axis, [(i, (i + step) % size) for i in range(size)])  59.2 us
    dot_general x12, matrix products, dot(): lax.dot_general(left, right, (dims, ((), ())), preferred_element_type=WIDE)  36.3 us
    ppermute x12, starting transfers between devices, send_split(): return lax.ppermute(block, DATA, pairs)  23 us
    ppermute x7, waiting for transfers between devices, sum_everywhere(): lax.ppermute(values, axis, [(i, i ^ apart) for i in range(size)])  19.3 us
    unnamed x140, local copies, waits for them, and re-layouts  17.6 us
    ppermute x12, waiting for transfers between devices, send_split(): return lax.ppermute(block, DATA, pairs)  13.3 us
    sub x1, matrix products, on_device(): exponent = jnp.exp(scores - row_max)  11.1 us
  transfers between devices with their start and end apart: 63, of which 36 were waited for; matrix products, arithmetic and copies ran while one was open for 38% of the time, Pallas kernels for 1%

profile of v2, /device:TPU:0, one launch (start us, length us, event | category | flops | bytes accessed | tf_op | source)
XLA Modules:
  0.0 385.5 jit_solution(8372973794606350711)
XLA Ops:
  7.3 4.2 %collective-permute-start = (bf16[256,1024]{1,0:T(8,128)(2,1)}, bf16[256,1024]{1,0:T(8,128)(2,1)}, u32[]{:S(2)}, u32[]{:S(2)}) collective-permute-start(bf16[256,1024]{1,0:T(8,128)(2,1)} %param.18), channel_id=1, source_target_pairs={{0,3},{1,0},{2,1},{3,2},{4,7},{5,4},{6,5},{7,6},{8,11},{9,8},{10,9... | collective-permute-start | bytes 1572872 | tf_op jit(solution)/shard_map/ppermute | solution.py:30
  14.1 4.7 %collective-permute-start.5 = (bf16[8,1920]{1,0:T(8,128)(2,1)S(1)}, bf16[8,1920]{1,0:T(8,128)(2,1)S(1)}, u32[]{:S(2)}, u32[]{:S(2)}) collective-permute-start(bf16[8,1920]{1,0:T(8,128)(2,1)S(1)} %get-tuple-element.118), channel_id=1, source_target_pairs={{0,2},{1,3},{2,0},{3,1},{4,6},{5,7},{6,4},{7,5},{8,10},{9,11},{10,... | collective-permute-start | bytes 92168 | tf_op jit(solution)/shard_map/ppermute | solution.py:30
  29.6 3.1 collective-permute-start.9
  40.1 3.2 collective-permute-start.12
  63.6 3.7 add_convert_fusion.1
  68.4 11.1 %fusion.104 = (f32[4,1024]{1,0:T(4,128)S(1)}, f32[4,1024,1024]{1,2,0:T(8,128)}) fusion(pred[1024,1024]{0,1:T(8,128)(4,1)} %broadcast_compare_fusion, bf16[1024,4,64]{0,2,1:T(8,128)(2,1)} %bitcast.244, bf16[1024,4,64]{0,2,1:T(8,128)(2,1)S(1)} %bitcast.242), kind=kOutput, calls=%fused_computation.293 | convolution fusion | flops 553649152 | bytes 18890752 | tf_op jit(solution)/shard_map/sub | solution.py:304
  79.5 7.9 %fusion.23 = bf16[4,64,1024]{2,1,0:T(8,128)(2,1)S(1)} fusion(bf16[1024,4,64]{0,2,1:T(8,128)(2,1)} %bitcast.254, f32[4,1024,1024]{1,2,0:T(8,128)} %get-tuple-element.144, f32[4,1024]{1,0:T(4,128)S(1)} %get-tuple-element.143), kind=kOutput, calls=%fused_computation.51 | convolution fusion | flops 545521664 | bytes 17842176 | tf_op jit(solution)/shard_map/hqk,khd->qhd/dot_general | solution.py:307
  88.9 2.8 collective-permute-start.17
  91.6 4.5 %collective-permute-done.15 = bf16[128,1024]{1,0:T(8,128)(2,1)S(1)} collective-permute-done((bf16[128,1024]{1,0:T(8,128)(2,1)S(1)}, bf16[128,1024]{1,0:T(8,128)(2,1)S(1)}, u32[]{:S(2)}, u32[]{:S(2)}) %collective-permute-start.15) | collective-permute-done | bytes 262176 | tf_op jit(solution)/shard_map/ppermute | solution.py:30
  96.4 3.1 collective-permute-start.18
  99.6 3.2 collective-permute-start.27
  103.3 8.6 %collective-permute-done.18 = bf16[256,1024]{1,0:T(8,128)(2,1)S(1)} collective-permute-done((bf16[256,1024]{1,0:T(8,128)(2,1)S(1)}, bf16[256,1024]{1,0:T(8,128)(2,1)S(1)}, u32[]{:S(2)}, u32[]{:S(2)}) %collective-permute-start.18) | collective-permute-done | bytes 524320 | tf_op jit(solution)/shard_map/ppermute | solution.py:30
  111.9 3.8 collective-permute-done.16
  117.6 9.3 %collective-permute-done.28 = bf16[256,1024]{1,0:T(8,128)(2,1)S(1)} collective-permute-done((bf16[256,1024]{1,0:T(8,128)(2,1)S(1)}, bf16[256,1024]{1,0:T(8,128)(2,1)S(1)}, u32[]{:S(2)}, u32[]{:S(2)}) %collective-permute-start.28) | collective-permute-done | bytes 524320 | tf_op jit(solution)/shard_map/ppermute | solution.py:30
  128.7 3.1 collective-permute-start.30
  134.6 4.7 %collective-permute-done.29 = bf16[128,1024]{1,0:T(8,128)(2,1)S(1)} collective-permute-done((bf16[128,1024]{1,0:T(8,128)(2,1)}, bf16[128,1024]{1,0:T(8,128)(2,1)S(1)}, u32[]{:S(2)}, u32[]{:S(2)}) %collective-permute-start.29) | collective-permute-done | bytes 262176 | tf_op jit(solution)/shard_map/ppermute | solution.py:30
  144.7 3.3 collective-permute-start.22
  157.3 4.5 %multiply_convert_fusion.1 = (bf16[1024,1024]{1,0:T(8,128)(2,1)S(1)}, f32[1024,1024]{1,0:T(8,128)S(1)}) fusion(f32[1024]{0:T(1024)S(1)} %bitcast.295, bf16[1024,1024]{1,0:T(8,128)(2,1)} %constant_dynamic-update-slice_fusion.13, bf16[1024,1024]{1,0:T(8,128)(2,1)S(1)} %bitcast.240), kind=kOutput, calls=%fused_computation.26 | convolution fusion | flops 2153775104 | bytes 10489856 | tf_op jit(solution)/shard_map/dot_general | solution.py:207
  161.8 4.0 %convert_reduce_fusion.1 = (f32[1024]{0:T(1024)S(1)}, bf16[1024,1024]{1,0:T(8,128)(2,1)S(1)}) fusion(f32[1024,1024]{1,0:T(8,128)S(1)} %get-tuple-element.150, f32[1024]{0:T(1024)S(1)} %bitcast.296, bf16[1024,1024]{1,0:T(8,128)(2,1)S(1)} %copy-done.37, bf16[1024,1024]{1,0:T(8,128)(2,1)S(1)} %bitcast.246), kind=kOutput, calls=%fused_computation.24 | convolution fusion | flops 2161114112 | bytes 10493952 | tf_op jit(solution)/shard_map/dot_general | solution.py:207
  168.4 3.8 collective-permute-start.33
  174.7 3.4 collective-permute-start.25
  179.5 3.4 collective-permute-start.34
  183.0 4.0 %convolution_convert_fusion.1 = bf16[1024,1024]{1,0:T(8,128)(2,1)S(1)} fusion(bf16[1024,1024]{1,0:T(8,128)(2,1)} %constant_dynamic-update-slice_fusion.13, bf16[1024,1024]{1,0:T(8,128)(2,1)S(1)} %get-tuple-element.157), kind=kOutput, calls=%fused_computation.42 | convolution fusion | flops 2148532224 | bytes 6291456 | tf_op jit(solution)/shard_map/dot_general | solution.py:207
  187.3 3.3 collective-permute-start.26
  190.7 5.4 %collective-permute-done.34 = bf16[256,1024]{1,0:T(8,128)(2,1)S(1)} collective-permute-done((bf16[256,1024]{1,0:T(8,128)(2,1)S(1)}, bf16[256,1024]{1,0:T(8,128)(2,1)S(1)}, u32[]{:S(2)}, u32[]{:S(2)}) %collective-permute-start.34) | collective-permute-done | bytes 524320 | tf_op jit(solution)/shard_map/ppermute | solution.py:30
  198.5 4.4 %collective-permute-done.26 = bf16[256,1024]{1,0:T(8,128)(2,1)S(1)} collective-permute-done((bf16[256,1024]{1,0:T(8,128)(2,1)S(1)}, bf16[256,1024]{1,0:T(8,128)(2,1)S(1)}, u32[]{:S(2)}, u32[]{:S(2)}) %collective-permute-start.26) | collective-permute-done | bytes 524320 | tf_op jit(solution)/shard_map/ppermute | solution.py:30
  205.5 3.2 collective-permute-start.35
  211.4 2.8 pad_maximum_fusion.1
  214.1 3.6 collective-permute-done.36
  217.9 3.5 collective-permute-start.38
  222.5 2.9 collective-permute-done.37
  228.5 9.8 %fusion.26 = bf16[4,64,1024]{2,1,0:T(8,128)(2,1)} fusion(bf16[1024,4,64]{0,2,1:T(8,128)(2,1)S(1)} %bitcast.301, f32[4,1024,1024]{1,2,0:T(8,128)} %get-tuple-element.144, f32[4,1024]{1,0:T(4,128)S(1)} %get-tuple-element.143), kind=kOutput, calls=%fused_computation.52 | convolution fusion | flops 545521664 | bytes 17842176 | tf_op jit(solution)/shard_map/hqk,qhd->khd/dot_general | solution.py:361
  239.0 9.8 %multiply_reduce_fusion = (f32[4,1024]{1,0:T(4,128)S(1)}, f32[4,1024,1024]{1,2,0:T(8,128)}) fusion(f32[4,1024,1024]{1,2,0:T(8,128)S(1)} %bitcast.221, f32[4,1024]{1,0:T(4,128)S(1)} %get-tuple-element.143, bf16[1024,4,64]{0,2,1:T(8,128)(2,1)} %bitcast.302, bf16[1024,4,64]{0,2,1:T(8,128)(2,1)} %bitcast.255), kind=kOutput, calls=%fused_computation.2 | convolution fusion | flops 549449728 | bytes 34635776 | tf_op jit(solution)/shard_map/qhd,khd->hqk/dot_general | solution.py:351
  248.8 7.9 %multiply_convert_fusion = bf16[4,1024,1024]{1,2,0:T(8,128)(2,1)S(1)} fusion(f32[4,1024,1024]{1,2,0:T(8,128)} %get-tuple-element.154, f32[4,1024]{1,0:T(4,128)S(1)} %get-tuple-element.153, f32[4,1024,1024]{1,2,0:T(8,128)S(1)} %bitcast.221, f32[4,1024]{1,0:T(4,128)S(1)} %get-tuple-element.143), kind=kLoop, calls=%fused_computation.1 | loop fusion | flops 16777216 | bytes 41975808 | tf_op jit(solution)/shard_map/convert_element_type | solution.py:353
  261.3 6.6 %fusion.85 = (f32[1024]{0:T(1024)S(1)}, f32[1024]{0:T(1024)S(1)}, bf16[1024,1024]{1,0:T(8,128)(2,1)}, f32[1024,1024]{1,0:T(8,128)}, f32[1024,1024]{1,0:T(8,128)}) fusion(f32[1024]{0:T(1024)S(1)} %add_rsqrt_fusion, f32[1024]{0:T(1024)S(1)} %broadcast_multiply_fusion.2, bf16[1024,1024]{1,0:T(8,128)(2,1)S(1)} %constant_dynamic-update-slice_fusion, ...), kind=kOutput, calls=%fused_computation.278 | convolution fusion | flops 1622669312 | bytes 15745024 | tf_op jit(solution)/shard_map/dot_general | solution.py:207
  268.0 4.0 %copy.74 = bf16[1024,1024]{1,0:T(8,128)(2,1)} copy(bf16[1024,1024]{0,1:T(8,128)(2,1)} %bitcast.226) | data formatting | bytes 4194304 | tf_op jit(solution)/shard_map/dot_general | solution.py:207
  280.4 2.9 copy-done.28
  290.1 6.3 %collective-permute-start.45 = (bf16[4,2,16,1152]{3,2,1,0:T(8,128)(2,1)S(1)}, bf16[4,2,16,1152]{3,2,1,0:T(8,128)(2,1)S(1)}, u32[]{:S(2)}, u32[]{:S(2)}) collective-permute-start(bf16[4,2,16,1152]{3,2,1,0:T(8,128)(2,1)S(1)} %get-tuple-element.24), channel_id=1, source_target_pairs={{0,64},{4,20},{8,72},{12,28},{16,80},{20,4},{24,88},{28,12},{32,96... | collective-permute-start | bytes 884744 | tf_op jit(solution)/shard_map/ppermute | solution.py:80
  299.6 4.6 %collective-permute-done.45 = bf16[4,2,16,1152]{3,2,1,0:T(8,128)(2,1)S(1)} collective-permute-done((bf16[4,2,16,1152]{3,2,1,0:T(8,128)(2,1)S(1)}, bf16[4,2,16,1152]{3,2,1,0:T(8,128)(2,1)S(1)}, u32[]{:S(2)}, u32[]{:S(2)}) %collective-permute-start.45) | collective-permute-done | bytes 294944 | tf_op jit(solution)/shard_map/ppermute | solution.py:80
  304.6 3.2 collective-permute-start.49
  307.8 2.8 collective-permute-start.48
  323.0 9.3 %collective-permute-done.52 = f32[8,1920]{1,0:T(8,128)S(1)} collective-permute-done((f32[8,1920]{1,0:T(8,128)S(1)}, f32[8,1920]{1,0:T(8,128)S(1)}, u32[]{:S(2)}, u32[]{:S(2)}) %collective-permute-start.52) | collective-permute-done | bytes 61472 | tf_op jit(solution)/shard_map/ppermute | solution.py:30
  334.0 5.3 %stack.170 = f32[8]{0:T(128)S(1)} concatenate(f32[1]{0:T(128)} %bitcast.58, f32[1]{0:T(128)} %bitcast.59, f32[1]{0:T(128)} %bitcast.60, f32[1]{0:T(128)} %bitcast.61, f32[1]{0:T(128)} %bitcast.108, f32[1]{0:T(128)} %bitcast.114, f32[1]{0:T(128)} %bitcast.120, f32[1]{0:T(128)} %bitcast.123), dimensions={0} | concatenate | bytes 64 | tf_op jit(solution)/shard_map/stack | solution.py:428
  340.7 4.2 %collective-permute-done.55 = f32[8,128]{0,1:T(8,128)S(1)} collective-permute-done((f32[8,128]{0,1:T(8,128)S(1)}, f32[8,128]{0,1:T(8,128)S(1)}, u32[]{:S(2)}, u32[]{:S(2)}) %collective-permute-start.55) | collective-permute-done | bytes 4128 | tf_op jit(solution)/shard_map/ppermute | solution.py:174
  351.6 3.9 %collective-permute-done.57 = f32[8,128]{0,1:T(8,128)S(1)} collective-permute-done((f32[8,128]{0,1:T(8,128)S(1)}, f32[8,128]{0,1:T(8,128)S(1)}, u32[]{:S(2)}, u32[]{:S(2)}) %collective-permute-start.57) | collective-permute-done | bytes 4128 | tf_op jit(solution)/shard_map/ppermute | solution.py:174
  355.5 3.2 collective-permute-start.58
  358.7 2.7 collective-permute-done.58
  367.5 4.0 %collective-permute-done.60 = f32[8,128]{0,1:T(8,128)S(1)} collective-permute-done((f32[8,128]{0,1:T(8,128)S(1)}, f32[8,128]{0,1:T(8,128)S(1)}, u32[]{:S(2)}, u32[]{:S(2)}) %collective-permute-start.60) | collective-permute-done | bytes 4128 | tf_op jit(solution)/shard_map/ppermute | solution.py:174
  (378 shorter events, 138.8 us)
Async XLA Ops:
  7.2 147.2 %all-gather.3.cloned.1.call-start = ((), (), s32[]{:S(2)}) async-start(), calls=%async_computation.2 | async-start | bytes 4325376 | tf_op jit(solution)/shard_map/all_gather | solution.py:272
  7.3 39.8 %collective-permute-start = (bf16[256,1024]{1,0:T(8,128)(2,1)}, bf16[256,1024]{1,0:T(8,128)(2,1)}, u32[]{:S(2)}, u32[]{:S(2)}) collective-permute-start(bf16[256,1024]{1,0:T(8,128)(2,1)} %param.18), channel_id=1, source_target_pairs={{0,3},{1,0},{2,1},{3,2},{4,7},{5,4},{6,5},{7,6},{8,11},{9,8},{10,9... | collective-permute-start | bytes 1572872 | tf_op jit(solution)/shard_map/ppermute | solution.py:30
  11.4 37.0 %collective-permute-start.1 = (bf16[256,1024]{1,0:T(8,128)(2,1)}, bf16[256,1024]{1,0:T(8,128)(2,1)}, u32[]{:S(2)}, u32[]{:S(2)}) collective-permute-start(bf16[256,1024]{1,0:T(8,128)(2,1)} %param.18), channel_id=1, source_target_pairs={{0,1},{1,2},{2,3},{3,0},{4,5},{5,6},{6,7},{7,4},{8,9},{9,10},{10,1... | collective-permute-start | bytes 1572872 | tf_op jit(solution)/shard_map/ppermute | solution.py:30
  14.0 13.5 %collective-permute-start.6 = (bf16[8,1920]{1,0:T(8,128)(2,1)S(1)}, bf16[8,1920]{1,0:T(8,128)(2,1)S(1)}, u32[]{:S(2)}, u32[]{:S(2)}) collective-permute-start(bf16[8,1920]{1,0:T(8,128)(2,1)S(1)} %get-tuple-element.116), channel_id=1, source_target_pairs={{0,1},{1,2},{2,3},{3,0},{4,5},{5,6},{6,7},{7,4},{8,9},{9,10},{10,1... | collective-permute-start | bytes 92168 | tf_op jit(solution)/shard_map/ppermute | solution.py:30
  14.1 12.2 %collective-permute-start.5 = (bf16[8,1920]{1,0:T(8,128)(2,1)S(1)}, bf16[8,1920]{1,0:T(8,128)(2,1)S(1)}, u32[]{:S(2)}, u32[]{:S(2)}) collective-permute-start(bf16[8,1920]{1,0:T(8,128)(2,1)S(1)} %get-tuple-element.118), channel_id=1, source_target_pairs={{0,2},{1,3},{2,0},{3,1},{4,6},{5,7},{6,4},{7,5},{8,10},{9,11},{10,... | collective-permute-start | bytes 92168 | tf_op jit(solution)/shard_map/ppermute | solution.py:30
  29.6 5.9 %collective-permute-start.9 = (bf16[2,16,1152]{2,1,0:T(8,128)(2,1)S(1)}, bf16[2,16,1152]{2,1,0:T(8,128)(2,1)S(1)}, u32[]{:S(2)}, u32[]{:S(2)}) collective-permute-start(bf16[2,16,1152]{2,1,0:T(8,128)(2,1)S(1)} %fusion.57), channel_id=1, source_target_pairs={{0,64},{4,20},{8,72},{12,28},{16,80},{20,4},{24,88},{28,12},{32,96... | collective-permute-start | bytes 221192 | tf_op jit(solution)/shard_map/ppermute | solution.py:80
  40.1 11.0 %collective-permute-start.12 = (bf16[4,2,16,1152]{3,2,1,0:T(8,128)(2,1)}, bf16[4,2,16,1152]{3,2,1,0:T(8,128)(2,1)S(1)}, u32[]{:S(2)}, u32[]{:S(2)}) collective-permute-start(bf16[4,2,16,1152]{3,2,1,0:T(8,128)(2,1)} %get-tuple-element.109), channel_id=1, source_target_pairs={{0,16},{4,68},{8,24},{12,76},{16,0},{20,84},{24,8},{28,92},{32,48}... | collective-permute-start | bytes 884744 | tf_op jit(solution)/shard_map/ppermute | solution.py:80
  43.3 8.8 %collective-permute-start.11 = (bf16[4,2,16,1152]{3,2,1,0:T(8,128)(2,1)}, bf16[4,2,16,1152]{3,2,1,0:T(8,128)(2,1)S(1)}, u32[]{:S(2)}, u32[]{:S(2)}) collective-permute-start(bf16[4,2,16,1152]{3,2,1,0:T(8,128)(2,1)} %get-tuple-element.109), channel_id=1, source_target_pairs={{0,24},{4,100},{8,0},{12,108},{16,8},{20,116},{24,16},{28,124},{32... | collective-permute-start | bytes 884744 | tf_op jit(solution)/shard_map/ppermute | solution.py:80
  44.4 8.1 %collective-permute-start.13 = (bf16[4,2,16,1152]{3,2,1,0:T(8,128)(2,1)}, bf16[4,2,16,1152]{3,2,1,0:T(8,128)(2,1)S(1)}, u32[]{:S(2)}, u32[]{:S(2)}) collective-permute-start(bf16[4,2,16,1152]{3,2,1,0:T(8,128)(2,1)} %get-tuple-element.109), channel_id=1, source_target_pairs={{0,8},{4,36},{8,16},{12,44},{16,24},{20,52},{24,0},{28,60},{32,40}... | collective-permute-start | bytes 884744 | tf_op jit(solution)/shard_map/ppermute | solution.py:80
  47.0 268.8 %reduce-scatter.2.cloned.1.call-start = ((), (), s32[]{:S(2)}) async-start(), calls=%async_computation.1 | async-start | bytes 4325376 | tf_op jit(solution)/shard_map/reduce_scatter | solution.py:339
  48.0 9.1 %collective-permute-start.3 = (bf16[128,1024]{1,0:T(8,128)(2,1)S(1)}, bf16[128,1024]{1,0:T(8,128)(2,1)S(1)}, u32[]{:S(2)}, u32[]{:S(2)}) collective-permute-start(bf16[128,1024]{1,0:T(8,128)(2,1)S(1)} %slice.376), channel_id=1, source_target_pairs={{0,3},{1,0},{2,1},{3,2},{4,7},{5,4},{6,5},{7,6},{8,11},{9,8},{10,9... | collective-permute-start | bytes 786440 | tf_op jit(solution)/shard_map/ppermute | solution.py:30
  49.4 7.7 %collective-permute-start.2 = (bf16[128,1024]{1,0:T(8,128)(2,1)S(1)}, bf16[128,1024]{1,0:T(8,128)(2,1)S(1)}, u32[]{:S(2)}, u32[]{:S(2)}) collective-permute-start(bf16[128,1024]{1,0:T(8,128)(2,1)S(1)} %slice.375), channel_id=1, source_target_pairs={{0,1},{1,2},{2,3},{3,0},{4,5},{5,6},{6,7},{7,4},{8,9},{9,10},{10,1... | collective-permute-start | bytes 786440 | tf_op jit(solution)/shard_map/ppermute | solution.py:30
  88.3 7.8 %collective-permute-start.15 = (bf16[128,1024]{1,0:T(8,128)(2,1)S(1)}, bf16[128,1024]{1,0:T(8,128)(2,1)S(1)}, u32[]{:S(2)}, u32[]{:S(2)}) collective-permute-start(bf16[128,1024]{1,0:T(8,128)(2,1)S(1)} %get-tuple-element.92), channel_id=1, source_target_pairs={{0,1},{1,2},{2,3},{3,0},{4,5},{5,6},{6,7},{7,4},{8,9},{9,10},{10,1... | collective-permute-start | bytes 786440 | tf_op jit(solution)/shard_map/ppermute | solution.py:30
  88.9 7.3 %collective-permute-start.17 = (bf16[128,1024]{1,0:T(8,128)(2,1)S(1)}, bf16[128,1024]{1,0:T(8,128)(2,1)S(1)}, u32[]{:S(2)}, u32[]{:S(2)}) collective-permute-start(bf16[128,1024]{1,0:T(8,128)(2,1)S(1)} %get-tuple-element.93), channel_id=1, source_target_pairs={{0,3},{1,0},{2,1},{3,2},{4,7},{5,4},{6,5},{7,6},{8,11},{9,8},{10,9... | collective-permute-start | bytes 786440 | tf_op jit(solution)/shard_map/ppermute | solution.py:30
  96.4 15.5 %collective-permute-start.18 = (bf16[256,1024]{1,0:T(8,128)(2,1)S(1)}, bf16[256,1024]{1,0:T(8,128)(2,1)S(1)}, u32[]{:S(2)}, u32[]{:S(2)}) collective-permute-start(bf16[256,1024]{1,0:T(8,128)(2,1)S(1)} %pad_maximum_fusion.6), channel_id=1, source_target_pairs={{0,3},{1,0},{2,1},{3,2},{4,7},{5,4},{6,5},{7,6},{8,11},{9,8},{10,9... | collective-permute-start | bytes 1572872 | tf_op jit(solution)/shard_map/ppermute | solution.py:30
  99.6 16.1 %collective-permute-start.16 = (bf16[256,1024]{1,0:T(8,128)(2,1)S(1)}, bf16[256,1024]{1,0:T(8,128)(2,1)S(1)}, u32[]{:S(2)}, u32[]{:S(2)}) collective-permute-start(bf16[256,1024]{1,0:T(8,128)(2,1)S(1)} %pad_maximum_fusion.5), channel_id=1, source_target_pairs={{0,1},{1,2},{2,3},{3,0},{4,5},{5,6},{6,7},{7,4},{8,9},{9,10},{10,1... | collective-permute-start | bytes 1572872 | tf_op jit(solution)/shard_map/ppermute | solution.py:30
  99.6 28.0 %collective-permute-start.27 = (bf16[256,1024]{1,0:T(8,128)(2,1)S(1)}, bf16[256,1024]{1,0:T(8,128)(2,1)S(1)}, u32[]{:S(2)}, u32[]{:S(2)}) collective-permute-start(bf16[256,1024]{1,0:T(8,128)(2,1)S(1)} %copy-done.13), channel_id=1, source_target_pairs={{0,3},{1,0},{2,1},{3,2},{4,7},{5,4},{6,5},{7,6},{8,11},{9,8},{10,9... | collective-permute-start | bytes 1572872 | tf_op jit(solution)/shard_map/ppermute | solution.py:30
  102.9 24.1 %collective-permute-start.28 = (bf16[256,1024]{1,0:T(8,128)(2,1)S(1)}, bf16[256,1024]{1,0:T(8,128)(2,1)S(1)}, u32[]{:S(2)}, u32[]{:S(2)}) collective-permute-start(bf16[256,1024]{1,0:T(8,128)(2,1)S(1)} %copy-done.13), channel_id=1, source_target_pairs={{0,1},{1,2},{2,3},{3,0},{4,5},{5,6},{6,7},{7,4},{8,9},{9,10},{10,1... | collective-permute-start | bytes 1572872 | tf_op jit(solution)/shard_map/ppermute | solution.py:30
  117.6 24.1 %collective-permute-start.20 = (bf16[256,1024]{1,0:T(8,128)(2,1)}, bf16[256,1024]{1,0:T(8,128)(2,1)}, u32[]{:S(2)}, u32[]{:S(2)}) collective-permute-start(bf16[256,1024]{1,0:T(8,128)(2,1)} %get-tuple-element.63), channel_id=1, source_target_pairs={{0,1},{1,2},{2,3},{3,0},{4,5},{5,6},{6,7},{7,4},{8,9},{9,10},{10,1... | collective-permute-start | bytes 1572872 | tf_op jit(solution)/shard_map/ppermute | solution.py:30
  127.7 11.7 %collective-permute-start.29 = (bf16[128,1024]{1,0:T(8,128)(2,1)}, bf16[128,1024]{1,0:T(8,128)(2,1)S(1)}, u32[]{:S(2)}, u32[]{:S(2)}) collective-permute-start(bf16[128,1024]{1,0:T(8,128)(2,1)} %slice.410), channel_id=1, source_target_pairs={{0,1},{1,2},{2,3},{3,0},{4,5},{5,6},{6,7},{7,4},{8,9},{9,10},{10,1... | collective-permute-start | bytes 786440 | tf_op jit(solution)/shard_map/ppermute | solution.py:30
  128.7 11.4 %collective-permute-start.30 = (bf16[128,1024]{1,0:T(8,128)(2,1)}, bf16[128,1024]{1,0:T(8,128)(2,1)}, u32[]{:S(2)}, u32[]{:S(2)}) collective-permute-start(bf16[128,1024]{1,0:T(8,128)(2,1)} %slice.411), channel_id=1, source_target_pairs={{0,3},{1,0},{2,1},{3,2},{4,7},{5,4},{6,5},{7,6},{8,11},{9,8},{10,9... | collective-permute-start | bytes 786440 | tf_op jit(solution)/shard_map/ppermute | solution.py:30
  131.8 11.9 %collective-permute-start.19 = (bf16[256,1024]{1,0:T(8,128)(2,1)}, bf16[256,1024]{1,0:T(8,128)(2,1)}, u32[]{:S(2)}, u32[]{:S(2)}) collective-permute-start(bf16[256,1024]{1,0:T(8,128)(2,1)} %get-tuple-element.63), channel_id=1, source_target_pairs={{0,3},{1,0},{2,1},{3,2},{4,7},{5,4},{6,5},{7,6},{8,11},{9,8},{10,9... | collective-permute-start | bytes 1572872 | tf_op jit(solution)/shard_map/ppermute | solution.py:30
  142.7 7.7 %collective-permute-start.21 = (bf16[128,1024]{1,0:T(8,128)(2,1)S(1)}, bf16[128,1024]{1,0:T(8,128)(2,1)S(1)}, u32[]{:S(2)}, u32[]{:S(2)}) collective-permute-start(bf16[128,1024]{1,0:T(8,128)(2,1)S(1)} %slice.397), channel_id=1, source_target_pairs={{0,1},{1,2},{2,3},{3,0},{4,5},{5,6},{6,7},{7,4},{8,9},{9,10},{10,1... | collective-permute-start | bytes 786440 | tf_op jit(solution)/shard_map/ppermute | solution.py:30
  144.7 7.2 %collective-permute-start.22 = (bf16[128,1024]{1,0:T(8,128)(2,1)S(1)}, bf16[128,1024]{1,0:T(8,128)(2,1)S(1)}, u32[]{:S(2)}, u32[]{:S(2)}) collective-permute-start(bf16[128,1024]{1,0:T(8,128)(2,1)S(1)} %slice.398), channel_id=1, source_target_pairs={{0,3},{1,0},{2,1},{3,2},{4,7},{5,4},{6,5},{7,6},{8,11},{9,8},{10,9... | collective-permute-start | bytes 786440 | tf_op jit(solution)/shard_map/ppermute | solution.py:30
  168.3 10.9 %collective-permute-start.31 = (bf16[128,1024]{1,0:T(8,128)(2,1)S(1)}, bf16[128,1024]{1,0:T(8,128)(2,1)S(1)}, u32[]{:S(2)}, u32[]{:S(2)}) collective-permute-start(bf16[128,1024]{1,0:T(8,128)(2,1)S(1)} %get-tuple-element.84), channel_id=1, source_target_pairs={{0,1},{1,2},{2,3},{3,0},{4,5},{5,6},{6,7},{7,4},{8,9},{9,10},{10,1... | collective-permute-start | bytes 786440 | tf_op jit(solution)/shard_map/ppermute | solution.py:30
  168.4 10.8 %collective-permute-start.33 = (bf16[128,1024]{1,0:T(8,128)(2,1)S(1)}, bf16[128,1024]{1,0:T(8,128)(2,1)S(1)}, u32[]{:S(2)}, u32[]{:S(2)}) collective-permute-start(bf16[128,1024]{1,0:T(8,128)(2,1)S(1)} %get-tuple-element.85), channel_id=1, source_target_pairs={{0,3},{1,0},{2,1},{3,2},{4,7},{5,4},{6,5},{7,6},{8,11},{9,8},{10,9... | collective-permute-start | bytes 786440 | tf_op jit(solution)/shard_map/ppermute | solution.py:30
  174.6 12.4 %collective-permute-start.23 = (bf16[128,1024]{1,0:T(8,128)(2,1)S(1)}, bf16[128,1024]{1,0:T(8,128)(2,1)S(1)}, u32[]{:S(2)}, u32[]{:S(2)}) collective-permute-start(bf16[128,1024]{1,0:T(8,128)(2,1)S(1)} %get-tuple-element.88), channel_id=1, source_target_pairs={{0,1},{1,2},{2,3},{3,0},{4,5},{5,6},{6,7},{7,4},{8,9},{9,10},{10,1... | collective-permute-start | bytes 786440 | tf_op jit(solution)/shard_map/ppermute | solution.py:30
  174.7 12.3 %collective-permute-start.25 = (bf16[128,1024]{1,0:T(8,128)(2,1)S(1)}, bf16[128,1024]{1,0:T(8,128)(2,1)S(1)}, u32[]{:S(2)}, u32[]{:S(2)}) collective-permute-start(bf16[128,1024]{1,0:T(8,128)(2,1)S(1)} %get-tuple-element.89), channel_id=1, source_target_pairs={{0,3},{1,0},{2,1},{3,2},{4,7},{5,4},{6,5},{7,6},{8,11},{9,8},{10,9... | collective-permute-start | bytes 786440 | tf_op jit(solution)/shard_map/ppermute | solution.py:30
  179.5 16.6 %collective-permute-start.34 = (bf16[256,1024]{1,0:T(8,128)(2,1)S(1)}, bf16[256,1024]{1,0:T(8,128)(2,1)S(1)}, u32[]{:S(2)}, u32[]{:S(2)}) collective-permute-start(bf16[256,1024]{1,0:T(8,128)(2,1)S(1)} %pad_maximum_fusion.10), channel_id=1, source_target_pairs={{0,3},{1,0},{2,1},{3,2},{4,7},{5,4},{6,5},{7,6},{8,11},{9,8},{10,9... | collective-permute-start | bytes 1572872 | tf_op jit(solution)/shard_map/ppermute | solution.py:30
  182.9 14.9 %collective-permute-start.32 = (bf16[256,1024]{1,0:T(8,128)(2,1)S(1)}, bf16[256,1024]{1,0:T(8,128)(2,1)S(1)}, u32[]{:S(2)}, u32[]{:S(2)}) collective-permute-start(bf16[256,1024]{1,0:T(8,128)(2,1)S(1)} %pad_maximum_fusion.9), channel_id=1, source_target_pairs={{0,1},{1,2},{2,3},{3,0},{4,5},{5,6},{6,7},{7,4},{8,9},{9,10},{10,1... | collective-permute-start | bytes 1572872 | tf_op jit(solution)/shard_map/ppermute | solution.py:30
  187.3 15.6 %collective-permute-start.26 = (bf16[256,1024]{1,0:T(8,128)(2,1)S(1)}, bf16[256,1024]{1,0:T(8,128)(2,1)S(1)}, u32[]{:S(2)}, u32[]{:S(2)}) collective-permute-start(bf16[256,1024]{1,0:T(8,128)(2,1)S(1)} %pad_maximum_fusion.8), channel_id=1, source_target_pairs={{0,3},{1,0},{2,1},{3,2},{4,7},{5,4},{6,5},{7,6},{8,11},{9,8},{10,9... | collective-permute-start | bytes 1572872 | tf_op jit(solution)/shard_map/ppermute | solution.py:30
  190.6 12.9 %collective-permute-start.24 = (bf16[256,1024]{1,0:T(8,128)(2,1)S(1)}, bf16[256,1024]{1,0:T(8,128)(2,1)S(1)}, u32[]{:S(2)}, u32[]{:S(2)}) collective-permute-start(bf16[256,1024]{1,0:T(8,128)(2,1)S(1)} %pad_maximum_fusion.7), channel_id=1, source_target_pairs={{0,1},{1,2},{2,3},{3,0},{4,5},{5,6},{6,7},{7,4},{8,9},{9,10},{10,1... | collective-permute-start | bytes 1572872 | tf_op jit(solution)/shard_map/ppermute | solution.py:30
  205.5 12.2 %collective-permute-start.36 = (bf16[256,1024]{1,0:T(8,128)(2,1)}, bf16[256,1024]{1,0:T(8,128)(2,1)S(1)}, u32[]{:S(2)}, u32[]{:S(2)}) collective-permute-start(bf16[256,1024]{1,0:T(8,128)(2,1)} %get-tuple-element.58), channel_id=1, source_target_pairs={{0,1},{1,2},{2,3},{3,0},{4,5},{5,6},{6,7},{7,4},{8,9},{9,10},{10,1... | collective-permute-start | bytes 1572872 | tf_op jit(solution)/shard_map/ppermute | solution.py:30
  205.5 12.3 %collective-permute-start.35 = (bf16[256,1024]{1,0:T(8,128)(2,1)}, bf16[256,1024]{1,0:T(8,128)(2,1)S(1)}, u32[]{:S(2)}, u32[]{:S(2)}) collective-permute-start(bf16[256,1024]{1,0:T(8,128)(2,1)} %get-tuple-element.58), channel_id=1, source_target_pairs={{0,3},{1,0},{2,1},{3,2},{4,7},{5,4},{6,5},{7,6},{8,11},{9,8},{10,9... | collective-permute-start | bytes 1572872 | tf_op jit(solution)/shard_map/ppermute | solution.py:30
  217.8 7.7 %collective-permute-start.37 = (bf16[128,1024]{1,0:T(8,128)(2,1)S(1)}, bf16[128,1024]{1,0:T(8,128)(2,1)S(1)}, u32[]{:S(2)}, u32[]{:S(2)}) collective-permute-start(bf16[128,1024]{1,0:T(8,128)(2,1)S(1)} %slice.419), channel_id=1, source_target_pairs={{0,1},{1,2},{2,3},{3,0},{4,5},{5,6},{6,7},{7,4},{8,9},{9,10},{10,1... | collective-permute-start | bytes 786440 | tf_op jit(solution)/shard_map/ppermute | solution.py:30
  217.9 7.5 %collective-permute-start.38 = (bf16[128,1024]{1,0:T(8,128)(2,1)S(1)}, bf16[128,1024]{1,0:T(8,128)(2,1)S(1)}, u32[]{:S(2)}, u32[]{:S(2)}) collective-permute-start(bf16[128,1024]{1,0:T(8,128)(2,1)S(1)} %slice.420), channel_id=1, source_target_pairs={{0,3},{1,0},{2,1},{3,2},{4,7},{5,4},{6,5},{7,6},{8,11},{9,8},{10,9... | collective-permute-start | bytes 786440 | tf_op jit(solution)/shard_map/ppermute | solution.py:30
  280.3 7.3 %collective-permute-start.43 = (bf16[2,16,16,1152]{3,2,1,0:T(8,128)(2,1)S(1)}, bf16[2,16,16,1152]{3,2,1,0:T(8,128)(2,1)S(1)}, u32[]{:S(2)}, u32[]{:S(2)}) collective-permute-start(bf16[2,16,16,1152]{3,2,1,0:T(8,128)(2,1)S(1)} %dynamic-slice_convert_fusion), channel_id=1, source_target_pairs={{0,4},{4,0},{1,5},{5,1},{2,6},{6,2},{3,7},{7,3},{8,12},{12,8},{9,1... | collective-permute-start | bytes 3538952 | tf_op jit(solution)/shard_map/ppermute | solution.py:30
  284.1 12.5 %collective-permute-start.39 = (bf16[128,1024]{1,0:T(8,128)(2,1)}, bf16[128,1024]{1,0:T(8,128)(2,1)S(1)}, u32[]{:S(2)}, u32[]{:S(2)}) collective-permute-start(bf16[128,1024]{1,0:T(8,128)(2,1)} %get-tuple-element.80), channel_id=1, source_target_pairs={{0,1},{1,2},{2,3},{3,0},{4,5},{5,6},{6,7},{7,4},{8,9},{9,10},{10,1... | collective-permute-start | bytes 786440 | tf_op jit(solution)/shard_map/ppermute | solution.py:30
  285.7 11.0 %collective-permute-start.41 = (bf16[128,1024]{1,0:T(8,128)(2,1)S(1)}, bf16[128,1024]{1,0:T(8,128)(2,1)}, u32[]{:S(2)}, u32[]{:S(2)}) collective-permute-start(bf16[128,1024]{1,0:T(8,128)(2,1)S(1)} %get-tuple-element.81), channel_id=1, source_target_pairs={{0,3},{1,0},{2,1},{3,2},{4,7},{5,4},{6,5},{7,6},{8,11},{9,8},{10,9... | collective-permute-start | bytes 786440 | tf_op jit(solution)/shard_map/ppermute | solution.py:30
  290.0 9.6 %collective-permute-start.44 = (bf16[4,2,16,1152]{3,2,1,0:T(8,128)(2,1)S(1)}, bf16[4,2,16,1152]{3,2,1,0:T(8,128)(2,1)S(1)}, u32[]{:S(2)}, u32[]{:S(2)}) collective-permute-start(bf16[4,2,16,1152]{3,2,1,0:T(8,128)(2,1)S(1)} %get-tuple-element.23), channel_id=1, source_target_pairs={{0,32},{4,12},{8,40},{12,20},{16,48},{20,28},{24,56},{28,4},{32,64... | collective-permute-start | bytes 884744 | tf_op jit(solution)/shard_map/ppermute | solution.py:80
  290.1 14.1 %collective-permute-start.45 = (bf16[4,2,16,1152]{3,2,1,0:T(8,128)(2,1)S(1)}, bf16[4,2,16,1152]{3,2,1,0:T(8,128)(2,1)S(1)}, u32[]{:S(2)}, u32[]{:S(2)}) collective-permute-start(bf16[4,2,16,1152]{3,2,1,0:T(8,128)(2,1)S(1)} %get-tuple-element.24), channel_id=1, source_target_pairs={{0,64},{4,20},{8,72},{12,28},{16,80},{20,4},{24,88},{28,12},{32,96... | collective-permute-start | bytes 884744 | tf_op jit(solution)/shard_map/ppermute | solution.py:80
  296.4 7.9 %collective-permute-start.46 = (bf16[4,2,16,1152]{3,2,1,0:T(8,128)(2,1)S(1)}, bf16[4,2,16,1152]{3,2,1,0:T(8,128)(2,1)S(1)}, u32[]{:S(2)}, u32[]{:S(2)}) collective-permute-start(bf16[4,2,16,1152]{3,2,1,0:T(8,128)(2,1)S(1)} %get-tuple-element.25), channel_id=1, source_target_pairs={{0,96},{4,28},{8,104},{12,4},{16,112},{20,12},{24,120},{28,20},{32... | collective-permute-start | bytes 884744 | tf_op jit(solution)/shard_map/ppermute | solution.py:80
  304.5 8.2 %collective-permute-start.47 = (bf16[2,16,1152]{2,1,0:T(8,128)(2,1)S(1)}, bf16[2,16,1152]{2,1,0:T(8,128)(2,1)S(1)}, u32[]{:S(2)}, u32[]{:S(2)}) collective-permute-start(bf16[2,16,1152]{2,1,0:T(8,128)(2,1)S(1)} %get-tuple-element.105), channel_id=1, source_target_pairs={{0,8},{4,36},{8,16},{12,44},{16,24},{20,52},{24,0},{28,60},{32,40}... | collective-permute-start | bytes 221192 | tf_op jit(solution)/shard_map/ppermute | solution.py:80
  304.6 8.1 %collective-permute-start.49 = (bf16[2,16,1152]{2,1,0:T(8,128)(2,1)S(1)}, bf16[2,16,1152]{2,1,0:T(8,128)(2,1)S(1)}, u32[]{:S(2)}, u32[]{:S(2)}) collective-permute-start(bf16[2,16,1152]{2,1,0:T(8,128)(2,1)S(1)} %get-tuple-element.106), channel_id=1, source_target_pairs={{0,24},{4,100},{8,0},{12,108},{16,8},{20,116},{24,16},{28,124},{32... | collective-permute-start | bytes 221192 | tf_op jit(solution)/shard_map/ppermute | solution.py:80
  310.6 36.1 %collective-permute-start.42 = (bf16[256,1024]{1,0:T(8,128)(2,1)S(1)}, bf16[256,1024]{1,0:T(8,128)(2,1)S(1)}, u32[]{:S(2)}, u32[]{:S(2)}) collective-permute-start(bf16[256,1024]{1,0:T(8,128)(2,1)S(1)} %pad_maximum_fusion.12), channel_id=1, source_target_pairs={{0,3},{1,0},{2,1},{3,2},{4,7},{5,4},{6,5},{7,6},{8,11},{9,8},{10,9... | collective-permute-start | bytes 1572872 | tf_op jit(solution)/shard_map/ppermute | solution.py:30
  313.9 32.9 %collective-permute-start.40 = (bf16[256,1024]{1,0:T(8,128)(2,1)S(1)}, bf16[256,1024]{1,0:T(8,128)(2,1)S(1)}, u32[]{:S(2)}, u32[]{:S(2)}) collective-permute-start(bf16[256,1024]{1,0:T(8,128)(2,1)S(1)} %pad_maximum_fusion.11), channel_id=1, source_target_pairs={{0,1},{1,2},{2,3},{3,0},{4,5},{5,6},{6,7},{7,4},{8,9},{9,10},{10,1... | collective-permute-start | bytes 1572872 | tf_op jit(solution)/shard_map/ppermute | solution.py:30
  316.9 15.4 %collective-permute-start.53 = (f32[8,1920]{1,0:T(8,128)S(1)}, f32[8,1920]{1,0:T(8,128)S(1)}, u32[]{:S(2)}, u32[]{:S(2)}) collective-permute-start(f32[8,1920]{1,0:T(8,128)S(1)} %get-tuple-element.110), channel_id=1, source_target_pairs={{0,1},{1,2},{2,3},{3,0},{4,5},{5,6},{6,7},{7,4},{8,9},{9,10},{10,1... | collective-permute-start | bytes 184328 | tf_op jit(solution)/shard_map/ppermute | solution.py:30
  320.2 12.0 %collective-permute-start.52 = (f32[8,1920]{1,0:T(8,128)S(1)}, f32[8,1920]{1,0:T(8,128)S(1)}, u32[]{:S(2)}, u32[]{:S(2)}) collective-permute-start(f32[8,1920]{1,0:T(8,128)S(1)} %get-tuple-element.113), channel_id=1, source_target_pairs={{0,2},{1,3},{2,0},{3,1},{4,6},{5,7},{6,4},{7,5},{8,10},{9,11},{10,... | collective-permute-start | bytes 184328 | tf_op jit(solution)/shard_map/ppermute | solution.py:30
  (72 other events, 1219.4 us)
Sparse Core Ops, SparseCore 0:
  47.1 41.5 all-gather.2
  214.3 81.9 reduce-scatter.1
